TPU v7x, 32 devices: a whole 2x2x4 slice. The times are simulated.
32 devices in a mesh: seq: 16 (over z, y, x), tp: 2 (over core).
Axes of the slice: x: 2, y: 2, z: 4, core: 2. Of those that a mesh axis runs over, the one named last changes fastest.
Arguments:
- slab: bfloat16 [6144, 5120], P('seq', 'tp'), may hold values from -6 to 6
- token_request: int32 [6144, 1], P('seq'), may hold values from 0 to 31; in each aligned block of 384 rows (0 to 383, 384 to 767, ...) at most 24 rows name the same one
- request_slot: int32 [32], replicated, may hold values from 0 to 31, each once
- new_states: bfloat16 [32, 3, 5120], P('seq', None, 'tp'), may hold values from -6 to 6
- cache_gain: float32 [5120], replicated, may hold values from 0.25 to 1.75
- query_gain: float32 [5120], replicated, may hold values from 0.25 to 1.75
- key_weight: bfloat16 [5120, 3072], P('seq', 'tp'), may hold values from -0.078125 to 0.078125
- value_weight: bfloat16 [5120, 3072], P('seq', 'tp'), may hold values from -0.078125 to 0.078125
- query_weight: bfloat16 [5120, 3072], P('seq', 'tp'), may hold values from -0.078125 to 0.078125
Outputs:
- attended: bfloat16 [32, 3, 3072], P('seq', None, 'tp')
Inputs may be any that keep to these rules, and one draw needn't show every extreme that they name: `token_request`: in each aligned block of 384 tokens no request is named more than 24 times. `request_slot`: each slot is named by exactly one request.
All inputs are finite; a program needn't handle non-finite values.
Results may differ from a plain program's by a relative error of at most 0.0084.
Values may be sent and summed in bfloat16 or wider, within the bound.
No kernel may reach another device: no remote copies, remote signals or barrier semaphores. Data moves between devices by JAX's collectives and lax.ppermute only.
A program may use at most 128 MiB of HBM per device.

v0:
```python
import math

import jax
import jax.numpy as jnp
from jax import lax
from jax.sharding import PartitionSpec as P

HEAD = 128


def scale_rows(hidden_rows, norm_gain):
    values = hidden_rows.astype(jnp.float32)
    factor = lax.rsqrt(jnp.mean(values * values, axis=-1, keepdims=True) + 1e-06)
    return (values * factor * norm_gain).astype(jnp.bfloat16)


def project(left_rows, shard_rows):
    return jnp.dot(left_rows, shard_rows, preferred_element_type=jnp.float32)


def on_device(
    slab,
    token_request,
    request_slot,
    new_states,
    cache_gain,
    query_gain,
    key_weight,
    value_weight,
    query_weight,
):
    seq_count = lax.axis_size("seq")
    slab_full, states_full = (
        lax.all_gather(slab, "tp", axis=1, tiled=True),
        lax.all_gather(new_states, "tp", axis=2, tiled=True),
    )
    per_device, step_count, model_width = states_full.shape
    decode_rows = per_device * step_count
    normed_slab = scale_rows(slab_full, cache_gain)
    normed_state = scale_rows(states_full, cache_gain).reshape(decode_rows, model_width)
    normed_query = scale_rows(states_full, query_gain).reshape(decode_rows, model_width)
    local_width = key_weight.shape[1]
    heads_local = local_width // HEAD
    tok_rows = slab.shape[0]
    pieces = (
        lax.all_gather(key_weight, "seq", axis=0, tiled=True),
        lax.all_gather(value_weight, "seq", axis=0, tiled=True),
    )
    spread = lax.all_to_all(normed_query, "seq", split_axis=1, concat_axis=0, tiled=True)
    queries = lax.psum_scatter(
        jnp.dot(spread, query_weight, preferred_element_type=jnp.float32),
        "seq",
        scatter_dimension=0,
        tiled=True,
    ).astype(jnp.bfloat16)
    slab_keys = project(normed_slab, pieces[0]).astype(jnp.bfloat16)
    slab_values = project(normed_slab, pieces[1]).astype(jnp.bfloat16)
    state_keys = project(normed_state, pieces[0]).astype(jnp.bfloat16)
    state_values = project(normed_state, pieces[1]).astype(jnp.bfloat16)
    requests = request_slot.shape[0]
    capacity = max(2, 2 * tok_rows // requests)
    matches = token_request == jnp.arange(requests, dtype=jnp.int32)[None, :]
    target = jnp.sum(jnp.where(matches, request_slot[None, :], 0), axis=1)
    indices = jnp.arange(tok_rows, dtype=jnp.int32)
    earlier = (target[:, None] == target[None, :]) & (indices[None, :] < indices[:, None])
    position = jnp.sum(earlier.astype(jnp.int32), axis=1)
    destination = target * capacity + position
    slot_ids = jnp.arange(requests * capacity, dtype=jnp.int32)
    landing = destination[None, :] == slot_ids[:, None]
    placement = landing.astype(jnp.bfloat16)
    occupied = jnp.sum(landing.astype(jnp.int32), axis=1)
    packed_keys = jnp.dot(placement, slab_keys, preferred_element_type=jnp.float32).astype(
        jnp.bfloat16
    )
    packed_values = jnp.dot(placement, slab_values, preferred_element_type=jnp.float32).astype(
        jnp.bfloat16
    )
    block_slots = per_device * capacity
    arrived_keys, arrived_values, arrived_occupied = (
        lax.all_to_all(
            packed_keys.reshape(seq_count, block_slots, local_width),
            "seq",
            split_axis=0,
            concat_axis=0,
            tiled=True,
        ),
        lax.all_to_all(
            packed_values.reshape(seq_count, block_slots, local_width),
            "seq",
            split_axis=0,
            concat_axis=0,
            tiled=True,
        ),
        lax.all_to_all(
            occupied.reshape(seq_count, block_slots), "seq", split_axis=0, concat_axis=0, tiled=True
        ),
    )
    score_scale = 1.0 / math.sqrt(HEAD)
    query_blocks = queries.reshape(per_device, step_count, heads_local, HEAD)
    cache_keys = arrived_keys.reshape(seq_count, per_device, capacity, heads_local, HEAD)
    cache_values = arrived_values.reshape(seq_count, per_device, capacity, heads_local, HEAD)
    present = jnp.transpose(
        arrived_occupied.reshape(seq_count, per_device, capacity), (1, 0, 2)
    ).astype(jnp.float32)
    cache_scores = (
        jnp.einsum(
            "rshe,nrche->rshnc", query_blocks, cache_keys, preferred_element_type=jnp.float32
        )
        * score_scale
    )
    cache_weights = jnp.exp(cache_scores) * present[:, None, None, :, :]
    own_keys = state_keys.reshape(per_device, step_count, heads_local, HEAD)
    own_values = state_values.reshape(per_device, step_count, heads_local, HEAD)
    own_scores = (
        jnp.einsum("rshe,rthe->rsht", query_blocks, own_keys, preferred_element_type=jnp.float32)
        * score_scale
    )
    step_ids = jnp.arange(step_count, dtype=jnp.int32)
    causal = (step_ids[None, :] <= step_ids[:, None]).astype(jnp.float32)
    own_weights = jnp.exp(own_scores) * causal[None, :, None, :]
    denominator = jnp.sum(cache_weights, axis=(3, 4)) + jnp.sum(own_weights, axis=3)
    cache_probs = (cache_weights / denominator[..., None, None]).astype(jnp.bfloat16)
    own_probs = (own_weights / denominator[..., None]).astype(jnp.bfloat16)
    attended = jnp.einsum(
        "rshnc,nrche->rshe", cache_probs, cache_values, preferred_element_type=jnp.float32
    )
    attended = attended + jnp.einsum(
        "rsht,rthe->rshe", own_probs, own_values, preferred_element_type=jnp.float32
    )
    return attended.reshape(per_device, step_count, local_width).astype(jnp.bfloat16)


def solution(mesh):
    placed = (
        P("seq", "tp"),
        P("seq", None),
        P(),
        P("seq", None, "tp"),
        P(),
        P(),
        P("seq", "tp"),
        P("seq", "tp"),
        P("seq", "tp"),
    )
    return jax.shard_map(
        on_device, mesh=mesh, in_specs=placed, out_specs=P("seq", None, "tp"), check_vma=False
    )
```

profile of v0, /device:TPU:0, one launch (start us, length us, event | category | flops | bytes accessed | tf_op | source)
XLA Modules:
  0.0 604.3 jit_solution(7862910008799806872)
XLA Ops:
  6.6 0.7 all-gather.4.cloned.1.call-update
  7.3 0.7 all-gather.8.cloned.1.call-update
  8.1 0.7 all-gather.6.cloned.1.call-update
  8.8 0.1 select_reduce_fusion
  8.9 0.2 convert_reduce_fusion.1
  9.1 0.2 convert_reduce_fusion
  9.4 0.7 all_to_all.32
  10.0 8.3 %all-to-all-start.3 = ((s32[16,1,48]{2,1,0:T(1,128)}), s32[16,1,48]{2,1,0:T(1,128)S(1)}, u32[]{:S(2)}, u32[]{:S(2)}) async-start(s32[16,1,48]{2,1,0:T(1,128)} %all_to_all.32), calls=%async_computation.3 | async-start | bytes 16384 | tf_op jit(solution)/shard_map/all_to_all | solution.py:94
  18.4 1.8 all_gather.15
  20.2 0.2 fusion.40
  20.4 0.2 fusion.39
  20.6 0.1 all_to_all.28
  20.7 0.7 copy.40
  21.4 3.6 all-gather.4.cloned.1.call-done
  25.0 3.0 fusion.1
  27.9 6.8 %all-to-all-start.2 = ((bf16[6,16,320]{2,0,1:T(8,128)(2,1)}), bf16[6,16,320]{2,0,1:T(8,128)(2,1)S(1)}, u32[]{:S(2)}, u32[]{:S(2)}) async-start(bf16[6,16,320]{2,0,1:T(8,128)(2,1)} %copy.40), calls=%async_computation.2 | async-start | bytes 196608 | tf_op jit(solution)/shard_map/all_to_all | solution.py:49
  34.7 176.0 %all-gather.8.cloned.1.call-done = bf16[5120,1536]{1,0:T(8,128)(2,1)} async-done(((bf16[320,1536]{1,0:T(8,128)(2,1)}), bf16[5120,1536]{1,0:T(8,128)(2,1)}) %all-gather.8.cloned.1.call-update) | async-done | bytes 15728656 | tf_op jit(solution)/shard_map/all_gather | solution.py:46
  210.7 14.2 %convolution_convert_fusion = bf16[768,1536]{1,0:T(8,128)(2,1)} fusion(bf16[5120,1536]{1,0:T(8,128)(2,1)} %all-gather.8.cloned.1.call-done, bf16[384,5120]{1,0:T(8,128)(2,1)} %all-gather.4.cloned.1.call-done, f32[5120]{0:T(1024)S(1)} %copy-done.3, f32[384]{0:T(512)S(1)} %add_rsqrt_fusion.1, s32[384]{0:T(512)S(1)} %multiply_add_fusion), kind=kOutput, calls=%fused_computation.5 | convolution fusion | flops 6955696128 | bytes 22043648 | tf_op jit(solution)/shard_map/dot_general | solution.py:72
  224.9 3.8 all-to-all-start.1
  228.7 208.7 %all-gather.6.cloned.1.call-done = bf16[5120,1536]{1,0:T(8,128)(2,1)} async-done(((bf16[320,1536]{1,0:T(8,128)(2,1)}), bf16[5120,1536]{1,0:T(8,128)(2,1)}) %all-gather.6.cloned.1.call-update) | async-done | bytes 15728656 | tf_op jit(solution)/shard_map/all_gather | solution.py:47
  437.4 14.1 %convolution_convert_fusion.1 = bf16[768,1536]{1,0:T(8,128)(2,1)} fusion(bf16[5120,1536]{1,0:T(8,128)(2,1)} %all-gather.6.cloned.1.call-done, bf16[384,5120]{1,0:T(8,128)(2,1)} %all-gather.4.cloned.1.call-done, f32[5120]{0:T(1024)S(1)} %copy-done.3, f32[384]{0:T(512)S(1)} %add_rsqrt_fusion.1, s32[384]{0:T(512)S(1)} %multiply_add_fusion), kind=kOutput, calls=%fused_computation.6 | convolution fusion | flops 6955696128 | bytes 22043648 | tf_op jit(solution)/shard_map/dot_general | solution.py:75
  451.5 4.6 all-to-all-start
  456.1 0.7 copy.44
  456.8 0.9 reshape.95
  457.7 0.6 dynamic-slice.4
  459.0 0.6 fusion.46
  459.5 0.7 all_to_all.31
  460.2 2.0 fusion.50
  462.3 76.0 %fusion = f32[8,1536]{1,0:T(8,128)S(1)} fusion(f32[96,1536]{1,0:T(8,128)} %fusion.50), kind=kCustom, calls=%all-reduce-scatter | all-reduce-scatter fusion | flops 196609 | bytes 639488
  538.3 0.6 convert.6
  538.9 3.6 collective-permute-start
  542.5 3.8 collective-permute-start.1
  546.3 6.1 %collective-permute-start.2 = (bf16[8,1536]{1,0:T(8,128)(2,1)}, bf16[8,1536]{1,0:T(8,128)(2,1)}, u32[]{:S(2)}, u32[]{:S(2)}) collective-permute-start(bf16[8,1536]{1,0:T(8,128)(2,1)} %convert.6), channel_id=1, source_target_pairs={{0,6},{2,8},{4,10},{6,12},{8,14},{10,16},{12,18},{14,20},{16,22},{... | collective-permute-start | bytes 73736
  552.4 0.6 slice
  553.0 1.9 collective-permute-start.3
  555.0 0.6 copy.43
  555.6 0.4 collective-permute-done.3
  556.0 7.1 %concatenate = bf16[38,1536]{1,0:T(8,128)(2,1)} concatenate(bf16[6,1536]{1,0:T(8,128)(2,1)} %collective-permute-done.3, bf16[8,1536]{1,0:T(8,128)(2,1)} %collective-permute-done.2, bf16[8,1536]{1,0:T(8,128)(2,1)S(1)} %collective-permute-done.1, bf16[8,1536]{1,0:T(8,128)(2,1)S(1)} %collective-permute-done, f32[8,1536]{1,0:T(8,128)S(1)} %fusion), dimensions={0} | concatenate | bytes 258048
  563.2 0.8 dynamic-slice_convert_fusion
  564.0 7.6 %convolution_convert_fusion.5 = bf16[6,1536]{1,0:T(8,128)(2,1)S(1)} fusion(bf16[6,5120]{1,0:T(8,128)(2,1)S(1)} %reshape.95, bf16[5120,1536]{1,0:T(8,128)(2,1)} %all-gather.8.cloned.1.call-done), kind=kOutput, calls=%fused_computation.14 | convolution fusion | flops 94381056 | bytes 15808512 | tf_op jit(solution)/shard_map/dot_general | solution.py:18
  571.7 7.6 %convolution_convert_fusion.4 = bf16[6,1536]{1,0:T(8,128)(2,1)S(1)} fusion(bf16[6,5120]{1,0:T(8,128)(2,1)S(1)} %reshape.95, bf16[5120,1536]{1,0:T(8,128)(2,1)} %all-gather.6.cloned.1.call-done), kind=kOutput, calls=%fused_computation.13 | convolution fusion | flops 94381056 | bytes 15808512 | tf_op jit(solution)/shard_map/dot_general | solution.py:18
  579.4 0.2 fusion.49
  579.5 3.0 reshape.93
  582.6 5.9 fusion.48
  588.6 5.4 reshape.91
  594.0 2.9 fusion.24
  596.9 0.2 fusion.31
  597.2 0.6 convert_element_type.97
  (40 shorter events, 0.5 us)
Async XLA Ops:
  6.5 453.7 %copy-start = (bf16[320,1536]{1,0:T(8,128)(2,1)S(1)}, bf16[320,1536]{1,0:T(8,128)(2,1)}, u32[]{:S(2)}) copy-start(bf16[320,1536]{1,0:T(8,128)(2,1)} %param.17) | copy-start | bytes 2949124
  6.5 2.2 copy-start.6
  6.5 2.3 copy-start.7
  6.5 11.8 %copy-start.1 = (bf16[2,3,2560]{2,0,1:T(2,128)(2,1)S(1)}, bf16[2,3,2560]{2,0,1:T(2,128)(2,1)}, u32[]{:S(2)}) copy-start(bf16[2,3,2560]{2,0,1:T(2,128)(2,1)} %param.12) | copy-start | bytes 92164
  6.5 13.9 %copy-start.3 = (f32[5120]{0:T(1024)S(1)}, f32[5120]{0:T(1024)}, u32[]{:S(2)}) copy-start(f32[5120]{0:T(1024)} %param.13) | copy-start | bytes 61444
  6.5 13.9 %copy-start.2 = (f32[5120]{0:T(1024)S(1)}, f32[5120]{0:T(1024)}, u32[]{:S(2)}) copy-start(f32[5120]{0:T(1024)} %param.14) | copy-start | bytes 61444
  6.6 18.4 %all-gather.4.cloned.1.call-start = ((), (), s32[]{:S(2)}) async-start(), calls=%async_computation.4 | async-start | bytes 5898240 | tf_op jit(solution)/shard_map/all_gather | solution.py:34
  7.3 203.4 %all-gather.8.cloned.1.call-start = ((), (), s32[]{:S(2)}) async-start(), calls=%async_computation.6 | async-start | bytes 16711680 | tf_op jit(solution)/shard_map/all_gather | solution.py:46
  8.0 429.3 %all-gather.6.cloned.1.call-start = ((), (), s32[]{:S(2)}) async-start(), calls=%async_computation.5 | async-start | bytes 16711680 | tf_op jit(solution)/shard_map/all_gather | solution.py:47
  10.0 17.9 %all-to-all-start.3 = ((s32[16,1,48]{2,1,0:T(1,128)}), s32[16,1,48]{2,1,0:T(1,128)S(1)}, u32[]{:S(2)}, u32[]{:S(2)}) async-start(s32[16,1,48]{2,1,0:T(1,128)} %all_to_all.32), calls=%async_computation.3 | async-start | bytes 16384 | tf_op jit(solution)/shard_map/all_to_all | solution.py:94
  27.9 197.0 %all-to-all-start.2 = ((bf16[6,16,320]{2,0,1:T(8,128)(2,1)}), bf16[6,16,320]{2,0,1:T(8,128)(2,1)S(1)}, u32[]{:S(2)}, u32[]{:S(2)}) async-start(bf16[6,16,320]{2,0,1:T(8,128)(2,1)} %copy.40), calls=%async_computation.2 | async-start | bytes 196608 | tf_op jit(solution)/shard_map/all_to_all | solution.py:49
  224.9 226.6 %all-to-all-start.1 = ((bf16[16,48,1536]{2,1,0:T(8,128)(2,1)}), bf16[16,48,1536]{2,1,0:T(8,128)(2,1)S(1)}, u32[]{:S(2)}, u32[]{:S(2)}) async-start(bf16[16,48,1536]{2,1,0:T(8,128)(2,1)} %bitcast.30), calls=%async_computation.1 | async-start | bytes 4718592 | tf_op jit(solution)/shard_map/all_to_all | solution.py:80
  451.5 6.2 %copy-start.8 = (u32[32]{0:T(128)S(1)}, u32[32]{0:T(128)}, u32[]{:S(2)}) copy-start(u32[32]{0:T(128)} %constant.20) | copy-start | bytes 388
  451.5 137.0 %all-to-all-start = ((bf16[16,48,1536]{2,1,0:T(8,128)(2,1)}), bf16[16,48,1536]{2,1,0:T(8,128)(2,1)}, u32[]{:S(2)}, u32[]{:S(2)}) async-start(bf16[16,48,1536]{2,1,0:T(8,128)(2,1)} %bitcast.29), calls=%async_computation | async-start | bytes 4718592 | tf_op jit(solution)/shard_map/all_to_all | solution.py:87
  538.9 17.1 %collective-permute-start = (bf16[8,1536]{1,0:T(8,128)(2,1)}, bf16[8,1536]{1,0:T(8,128)(2,1)S(1)}, u32[]{:S(2)}, u32[]{:S(2)}) collective-permute-start(bf16[8,1536]{1,0:T(8,128)(2,1)} %convert.6), channel_id=1, source_target_pairs={{0,2},{2,4},{4,6},{6,8},{8,10},{10,12},{12,14},{14,16},{16,18},{18... | collective-permute-start | bytes 73736
  542.5 13.6 %collective-permute-start.1 = (bf16[8,1536]{1,0:T(8,128)(2,1)}, bf16[8,1536]{1,0:T(8,128)(2,1)S(1)}, u32[]{:S(2)}, u32[]{:S(2)}) collective-permute-start(bf16[8,1536]{1,0:T(8,128)(2,1)} %convert.6), channel_id=1, source_target_pairs={{0,4},{2,6},{4,8},{6,10},{8,12},{10,14},{12,16},{14,18},{16,20},{1... | collective-permute-start | bytes 73736
  546.3 9.7 %collective-permute-start.2 = (bf16[8,1536]{1,0:T(8,128)(2,1)}, bf16[8,1536]{1,0:T(8,128)(2,1)}, u32[]{:S(2)}, u32[]{:S(2)}) collective-permute-start(bf16[8,1536]{1,0:T(8,128)(2,1)} %convert.6), channel_id=1, source_target_pairs={{0,6},{2,8},{4,10},{6,12},{8,14},{10,16},{12,18},{14,20},{16,22},{... | collective-permute-start | bytes 73736
  553.0 3.0 collective-permute-start.3
  571.7 7.7 %copy-start.5 = (f32[3,3]{0,1:T(4,128)S(1)}, f32[3,3]{0,1:T(4,128)}, u32[]{:S(2)}) copy-start(f32[3,3]{0,1:T(4,128)} %fusion.46) | copy-start | bytes 112
  579.3 3.3 copy-start.4
Sparse Core Ops, SparseCore 0:
  8.9 15.9 all-gather.3
  27.8 182.9 all-gather.7
  213.5 223.7 all-gather.5
where the time goes:
time: 606 us; the launch traced here: 604 us
  waiting for transfers between devices  391 us (65%)
  blocking collectives  77.9 us (13%)
  matrix products  54.8 us (9%)
  starting transfers between devices  39 us (6%)
  local copies, waits for them, and re-layouts  22.9 us (4%)
  between operations  14 us (2%)
    all_gather x1, waiting for transfers between devices, on_device(): lax.all_gather(value_weight, 'seq', axis=0, tiled=True)  209 us
    all_gather x1, waiting for transfers between devices, on_device(): lax.all_gather(key_weight, 'seq', axis=0, tiled=True)  176 us
    unnamed x1, blocking collectives  76 us
    unnamed x4, starting transfers between devices  15.4 us
    dot_general x2, matrix products, project(): return jnp.dot(left_rows, shard_rows, preferred_element_type=jnp.float32)  15.2 us
    dot_general x1, matrix products, on_device(): jnp.dot(placement, slab_keys, preferred_element_type=jnp.float32)  14.2 us
    dot_general x1, matrix products, on_device(): jnp.dot(placement, slab_values, preferred_element_type=jnp.float32)  14.1 us
  transfers between devices with their start and end apart: 11, of which 4 were waited for; matrix products, arithmetic and copies ran while one was open for 25% of the time, Pallas kernels for 0%

commit v1 on v0

v1 whole, which is shorter than its diff:
```python
import functools
import math

import jax
import jax.numpy as jnp
from jax import lax
from jax.experimental import pallas as pl
from jax.experimental.pallas import tpu as pltpu
from jax.sharding import PartitionSpec as P

HEAD = 128
PAIR = 2
SLOTS = 4
NT = (((1,), (1,)), ((), ()))
VMEM_LIMIT = 48 * 1024 * 1024


def params():
    return pltpu.CompilerParams(vmem_limit_bytes=VMEM_LIMIT)


def split(values):
    high = values.astype(jnp.bfloat16)
    return high, (values - high.astype(jnp.float32)).astype(jnp.bfloat16)


def swap_gather(values, axis, size, index, perm):
    if size == 1:
        return values[None]
    other = lax.ppermute(values, axis, perm)
    first = index == 0
    return jnp.stack([jnp.where(first, values, other), jnp.where(first, other, values)])


def put_lanes(ref, rows, values):
    for tile in range(ref.shape[0]):
        part = values[:, tile * 128 : (tile + 1) * 128]
        if part.shape[1] < 128:
            fill = jnp.zeros((part.shape[0], 128 - part.shape[1]), part.dtype)
            part = jnp.concatenate([part, fill], axis=1)
        ref[tile, rows, :] = part


def take_lanes(ref, rows, width):
    tiles = [ref[tile, rows, :] for tile in range(ref.shape[0])]
    return jnp.concatenate(tiles, axis=1)[:, :width]


def absorb_kernel(heads, q_ref, weight_ref, gain_ref, out_ref, rows_ref):
    count = q_ref.shape[0]
    gain = gain_ref[...]
    for head in range(heads):
        lanes = pl.ds(head * HEAD, HEAD)
        mixed = lax.dot_general(
            q_ref[:, lanes], weight_ref[:, lanes], NT, preferred_element_type=jnp.float32
        )
        put_lanes(rows_ref, pl.ds(head, count, stride=heads), mixed * gain)
    out_ref[...] = take_lanes(rows_ref, slice(None), out_ref.shape[1]).astype(jnp.bfloat16)


def score_kernel(slots, per_slot, qk_ref, x_ref, slot_ref, out_ref):
    x = x_ref[...]
    tokens = x.shape[0]
    slot = jnp.broadcast_to(slot_ref[0], (per_slot, tokens))
    depth = SLOTS * per_slot

    def step(group, scores):
        start = pl.multiple_of(group * depth, depth)
        part = lax.dot_general(
            qk_ref[pl.ds(start, depth), :], x, NT, preferred_element_type=jnp.float32
        )
        for j in range(SLOTS):
            here = slot == group * SLOTS + j
            scores = jnp.where(here, part[j * per_slot : (j + 1) * per_slot], scores)
        return scores

    scores = lax.fori_loop(
        0, slots // SLOTS, step, jnp.zeros((per_slot, tokens), jnp.float32), unroll=True
    )
    values = x.astype(jnp.float32)
    high, low = split(values * values)
    ones = jnp.ones((8, x.shape[1]), jnp.bfloat16)
    total = lax.dot_general(ones, high, NT, preferred_element_type=jnp.float32)
    total = total + lax.dot_general(ones, low, NT, preferred_element_type=jnp.float32)
    total_high, total_low = split(total)
    row = lax.broadcasted_iota(jnp.int32, total.shape, 0)
    total = jnp.where(row == 0, total_high, jnp.where(row == 1, total_low, 0.0))
    out_ref[0] = jnp.concatenate([scores, total], axis=0).astype(jnp.bfloat16)


def value_kernel(
    slots, per_slot, heads, w_ref, x_ref, slot_ref, weight_ref, gain_ref, out_ref, d_ref,
    w_all, p_ref, mixed_ref,
):
    blocks, _, width = w_ref.shape
    for b in range(blocks):
        w_all[:, b * width : (b + 1) * width] = w_ref[b]
    tokens = blocks * width
    slot = slot_ref[...]
    one_hot = (
        lax.broadcasted_iota(jnp.int32, (slots, tokens), 0) == slot
    ).astype(jnp.float32).astype(jnp.bfloat16)
    weights = w_all[:per_slot, :]
    total = lax.dot_general(weights, one_hot, NT, preferred_element_type=jnp.float32)
    d_ref[...] = total
    inverse = jnp.where(total > 0.0, 1.0 / jnp.where(total > 0.0, total, 1.0), 0.0)
    high, low = split(inverse)
    scale = jnp.dot(high, one_hot, preferred_element_type=jnp.float32)
    scale = scale + jnp.dot(low, one_hot, preferred_element_type=jnp.float32)
    extra = w_all[per_slot:, :].astype(jnp.float32)
    factor = extra[0:1] + extra[1:2]
    p_ref[...] = (weights.astype(jnp.float32) * scale * factor).astype(jnp.bfloat16)
    depth = SLOTS * per_slot
    gain = gain_ref[...]
    x = x_ref[...]

    def step(group, carry):
        p = p_ref[...]
        zero = jnp.zeros_like(p)
        wide = jnp.broadcast_to(slot, p.shape)
        rows = [jnp.where(wide == group * SLOTS + j, p, zero) for j in range(SLOTS)]
        mixed = jnp.dot(
            jnp.concatenate(rows, axis=0), x, preferred_element_type=jnp.float32
        )
        put_lanes(mixed_ref, pl.ds(pl.multiple_of(group * depth, depth), depth), mixed * gain)
        return carry

    lax.fori_loop(0, slots // SLOTS, step, 0)
    count = out_ref.shape[0]
    for head in range(heads):
        rows = take_lanes(mixed_ref, pl.ds(head, count, stride=heads), x.shape[1])
        rows = rows.astype(jnp.bfloat16)
        lanes = pl.ds(head * HEAD, HEAD)
        out_ref[:, lanes] = jnp.dot(
            rows, weight_ref[:, lanes], preferred_element_type=jnp.float32
        ).astype(jnp.bfloat16)


def on_device(
    slab, token_request, request_slot, new_states, cache_gain, query_gain,
    key_weight, value_weight, query_weight,
):
    f32, bf16 = jnp.float32, jnp.bfloat16
    seq, tp = lax.axis_size("seq"), lax.axis_size("tp")
    k, c = lax.axis_index("seq"), lax.axis_index("tp")
    tokens, half = slab.shape
    model = half * tp
    own = tokens // tp
    feat = model // seq
    pair = PAIR if seq % PAIR == 0 else 1
    shards = seq // pair
    wide = feat * pair
    x, m = k % pair, k // pair
    groups = [[pair * i + p for i in range(shards)] for p in range(pair)]
    x_perm = [(i, i ^ 1) for i in range(seq)]
    tp_perm = [(0, 1), (1, 0)]
    local_width = key_weight.shape[1]
    heads_local = local_width // HEAD
    heads = heads_local * tp
    per, steps, _ = new_states.shape
    slots = request_slot.shape[0]
    own_rows = per * steps
    rows = slots * steps
    per_slot = steps * heads
    scale = 1.0 / math.sqrt(HEAD)

    def over_tp(values):
        if tp == 2:
            return swap_gather(values, "tp", tp, c, tp_perm)
        return lax.all_gather(values, "tp", axis=0, tiled=False)

    cut = slab.reshape(tp, own, half)
    if tp == 2:
        mine = lax.dynamic_index_in_dim(cut, c, 0, keepdims=False)
        other = lax.ppermute(
            lax.dynamic_index_in_dim(cut, 1 - c, 0, keepdims=False), "tp", tp_perm
        )
        whole = jnp.stack([jnp.where(c == 0, mine, other), jnp.where(c == 0, other, mine)])
    else:
        whole = lax.all_to_all(cut, "tp", 0, 0, tiled=True)
    message = whole.reshape(tp, own, shards // tp, wide).transpose(0, 2, 1, 3)
    slab_in = lax.all_to_all(
        message.reshape(shards, own, wide), "seq", 0, 0, tiled=True, axis_index_groups=groups
    )

    requests = lax.dynamic_index_in_dim(token_request.reshape(tp, own), c, 0, keepdims=False)
    match = requests[None, :] == jnp.arange(slots, dtype=jnp.int32)[:, None]
    target = jnp.sum(jnp.where(match, request_slot[:, None], 0), axis=0)
    states = over_tp(new_states.reshape(own_rows, half)).transpose(1, 0, 2).reshape(own_rows, model)
    squares = states.astype(f32)
    own_factor = lax.rsqrt(jnp.mean(squares * squares, axis=-1, keepdims=True) + 1e-06)
    slot_rows = -(-own // feat)
    carried = jnp.pad(target.astype(bf16), (0, slot_rows * feat - own)).reshape(slot_rows, feat)
    sent = jnp.concatenate(
        [
            states.reshape(own_rows, seq, feat).transpose(1, 0, 2),
            jnp.broadcast_to(carried[None], (seq, slot_rows, feat)),
        ],
        axis=1,
    )
    got = lax.all_to_all(sent, "seq", 0, 0, tiled=True)
    state_part = got[:, :own_rows].reshape(rows, feat)
    slots_in = got[:, own_rows:].reshape(shards, pair, slot_rows * feat)[:, :, :own]
    slots_in = lax.dynamic_index_in_dim(slots_in, x, 1, keepdims=False).astype(jnp.int32)

    query_part = lax.dynamic_slice(query_gain, (k * feat,), (feat,))
    gained = (state_part.astype(f32) * query_part[None]).astype(bf16)
    partial = jnp.dot(gained, query_weight, preferred_element_type=f32).astype(bf16)
    partial = lax.all_to_all(
        partial.reshape(seq, own_rows, local_width), "seq", 0, 0, tiled=True
    )
    query = (jnp.sum(partial.astype(f32), axis=0) * own_factor).astype(bf16)
    queries = lax.all_to_all(
        jnp.broadcast_to(query[None], (seq, own_rows, local_width)), "seq", 0, 0, tiled=True
    ).reshape(rows, local_width)
    queries = over_tp(queries).transpose(1, 0, 2).reshape(rows, heads * HEAD)

    def gather_rows(weight):
        block = swap_gather(weight, "seq", pair, x, x_perm).reshape(wide, local_width)
        return over_tp(block).transpose(1, 0, 2).reshape(wide, heads * HEAD)

    keys_full, values_full = gather_rows(key_weight), gather_rows(value_weight)
    gain = lax.dynamic_slice(cache_gain, (m * wide,), (wide,)).reshape(1, wide)
    absorbed = pl.pallas_call(
        functools.partial(absorb_kernel, heads),
        out_shape=jax.ShapeDtypeStruct((rows * heads, wide), bf16),
        scratch_shapes=[pltpu.VMEM((-(-wide // 128), rows * heads, 128), f32)],
        compiler_params=params(),
        name="absorb",
    )(queries, keys_full, gain)

    new_cols = rows // shards
    width = -(-(own + new_cols) // 128) * 128
    state_wide = swap_gather(state_part, "seq", pair, x, x_perm)
    state_wide = state_wide.transpose(1, 0, 2).reshape(shards, new_cols, wide)
    tokens_in = jnp.concatenate(
        [slab_in, jnp.pad(state_wide, ((0, 0), (0, width - own - new_cols), (0, 0)))], axis=1
    ).reshape(shards * width, wide)

    group = x * tp + c
    new_slot = jnp.arange(rows, dtype=jnp.int32) // steps
    new_slot = jnp.where(new_slot % (pair * tp) == group, new_slot, -1).reshape(shards, new_cols)
    slot_in = jnp.concatenate(
        [slots_in, new_slot, jnp.full((shards, width - own - new_cols), -1, jnp.int32)], axis=1
    )

    out_rows = per_slot + 8
    partial = pl.pallas_call(
        functools.partial(score_kernel, slots, per_slot),
        grid=(shards,),
        in_specs=[
            pl.BlockSpec((rows * heads, wide), lambda i: (0, 0)),
            pl.BlockSpec((width, wide), lambda i: (i, 0)),
            pl.BlockSpec((1, 1, width), lambda i: (i, 0, 0)),
        ],
        out_specs=pl.BlockSpec((1, out_rows, width), lambda i: (i, 0, 0)),
        out_shape=jax.ShapeDtypeStruct((shards, out_rows, width), bf16),
        compiler_params=params(),
        name="scores",
    )(absorbed, tokens_in, slot_in.reshape(shards, 1, width))
    partial = lax.all_to_all(partial, "seq", 0, 0, tiled=True, axis_index_groups=groups)
    summed = jnp.sum(partial.astype(f32), axis=0)
    mean = (summed[per_slot] + summed[per_slot + 1]) / model
    factor = lax.rsqrt(mean + 1e-06)[None]
    my_slot = lax.dynamic_index_in_dim(slot_in, m, 0, keepdims=True)
    column = jnp.arange(width, dtype=jnp.int32)[None]
    step_of = jnp.arange(per_slot, dtype=jnp.int32)[:, None] // heads
    seen = (my_slot >= 0) & ((column < own) | ((column - own) % steps <= step_of))
    weights = jnp.where(seen, jnp.exp(summed[:per_slot] * (factor * scale)), 0.0)
    high, low = split(factor)
    ready = jnp.concatenate(
        [weights.astype(bf16), high, low, jnp.zeros((6, width), bf16)], axis=0
    )
    weights_in = lax.all_to_all(
        jnp.broadcast_to(ready[None], (shards, out_rows, width)),
        "seq", 0, 0, tiled=True, axis_index_groups=groups,
    )

    attended, totals = pl.pallas_call(
        functools.partial(value_kernel, slots, per_slot, heads),
        out_shape=(
            jax.ShapeDtypeStruct((rows, heads * HEAD), bf16),
            jax.ShapeDtypeStruct((per_slot, slots), f32),
        ),
        scratch_shapes=[
            pltpu.VMEM((out_rows, shards * width), bf16),
            pltpu.VMEM((per_slot, shards * width), bf16),
            pltpu.VMEM((-(-wide // 128), rows * heads, 128), f32),
        ],
        compiler_params=params(),
        name="values",
    )(weights_in, tokens_in, slot_in.reshape(1, shards * width), values_full, gain)

    totals = totals.T.reshape(seq, per, steps, tp, heads_local).transpose(0, 3, 1, 2, 4)
    totals = totals.reshape(seq, tp, 1, own_rows * heads_local)
    totals = jnp.concatenate(split(totals), axis=2)
    parts = attended.reshape(seq, own_rows, tp, local_width).transpose(0, 2, 1, 3)
    spare = local_width - own_rows * heads_local
    sent = jnp.concatenate([parts, jnp.pad(totals, ((0, 0), (0, 0), (0, 0), (0, spare)))], axis=2)
    got = lax.all_to_all(
        sent.reshape(seq * tp, own_rows + 2, local_width), ("seq", "tp"), 0, 0, tiled=True
    ).reshape(shards, pair, tp, own_rows + 2, local_width).astype(f32)
    sums = jnp.sum(got[:, :, :, :own_rows], axis=0)
    share = got[0, :, :, own_rows, :] + got[0, :, :, own_rows + 1, :]
    share = share[..., : own_rows * heads_local].reshape(pair, tp, own_rows, heads_local)
    share = share / jnp.sum(share, axis=(0, 1), keepdims=True)
    sums = sums.reshape(pair, tp, own_rows, heads_local, HEAD) * share[..., None]
    return jnp.sum(sums, axis=(0, 1)).reshape(per, steps, local_width).astype(bf16)


def solution(mesh):
    placed = (
        P("seq", "tp"),
        P("seq", None),
        P(),
        P("seq", None, "tp"),
        P(),
        P(),
        P("seq", "tp"),
        P("seq", "tp"),
        P("seq", "tp"),
    )
    return jax.shard_map(
        on_device, mesh=mesh, in_specs=placed, out_specs=P("seq", None, "tp"), check_vma=False
    )
```

time: 606 us -> 213 us (0.35)
  waiting for transfers between devices: 391 us -> 85.9 us
  blocking collectives: 77.9 us -> 23.1 us
  matrix products: 54.8 us -> 0.34 us
  Pallas kernels: 0 us -> 28.8 us
  other arithmetic: 5.06 us -> 21.9 us
  between operations: 14 us -> 0.5 us
  starting transfers between devices: 39 us -> 31.7 us
    all_gather x3 -> x0, waiting for transfers between devices: 388 us -> none  [the longest x1 209 us: on_device(): lax.all_gather(value_weight, 'seq', axis=0, tiled=True)]
    all_to_all x4 -> x6, waiting for transfers between devices: 0.01 us -> 82.4 us  [the longest x1 37.4 us: on_device(): lax.all_to_all(partial.reshape(seq, own_rows, local_width), 'seq', 0, 0,...]
    unnamed x1 -> x0, blocking collectives: 76 us -> none
    dot_general x9 -> x1, matrix products: 54.8 us -> 0.34 us  [on_device(): jnp.dot(gained, query_weight, preferred_element_type=f32).astype(bf16)]
    pallas_call x0 -> x3, Pallas kernels: none -> 28.8 us  [the longest x1 13.7 us: on_device(): pl.pallas_call(functools.partial(value_kernel, slots, per_slot, heads), o...]
    all_to_all x0 -> x1, blocking collectives: none -> 23.1 us  [on_device(): lax.all_to_all(sent.reshape(seq * tp, own_rows + 2, local_width), ('seq',...]
    unnamed x4 -> x0, starting transfers between devices: 15.4 us -> none
    another operation x0 -> x10, other arithmetic: none -> 12.4 us  [the longest x8 12.1 us: swap_gather(): jnp.stack([jnp.where(first, values, other), jnp.where(first, other, value...]
  transfers between devices with their start and end apart: 11 -> 14, of which waited for: 4 -> 7; matrix products, arithmetic and copies ran while one was open for 25% -> 14% of each run, Pallas kernels for 0% -> 2%
where the time goes in v1:
time: 213 us; the launch traced here: 212 us
  waiting for transfers between devices  85.9 us (40%)
  starting transfers between devices  31.7 us (15%)
  Pallas kernels  28.8 us (14%)
  blocking collectives  23.1 us (11%)
  other arithmetic  21.9 us (10%)
  local copies, waits for them, and re-layouts  19.3 us (9%)
    all_to_all x1, waiting for transfers between devices, on_device(): lax.all_to_all(partial.reshape(seq, own_rows, local_width), 'seq', 0, 0,...  37.4 us
    all_to_all x1, blocking collectives, on_device(): lax.all_to_all(sent.reshape(seq * tp, own_rows + 2, local_width), ('seq',...  23.1 us
    all_to_all x1, waiting for transfers between devices, on_device(): lax.all_to_all(message.reshape(shards, own, wide), 'seq', 0, 0, tiled=Tru...  20.2 us
    pallas_call x1, Pallas kernels, on_device(): pl.pallas_call(functools.partial(value_kernel, slots, per_slot, heads), o...  13.7 us
    another operation x8, other arithmetic, swap_gather(): jnp.stack([jnp.where(first, values, other), jnp.where(first, other, value...  12.1 us
    pallas_call x1, Pallas kernels, on_device(): pl.pallas_call(functools.partial(score_kernel, slots, per_slot), grid=(sh...  10.6 us
    all_to_all x1, waiting for transfers between devices, on_device(): lax.all_to_all(partial, 'seq', 0, 0, tiled=True, axis_index_groups=groups)  10.2 us
    all_to_all x1, starting transfers between devices, on_device(): got = lax.all_to_all(sent, 'seq', 0, 0, tiled=True)  7.88 us
  transfers between devices with their start and end apart: 14, of which 7 were waited for; matrix products, arithmetic and copies ran while one was open for 14% of the time, Pallas kernels for 2%

profile of v1, /device:TPU:0, one launch (start us, length us, event | category | flops | bytes accessed | tf_op | source)
XLA Modules:
  0.0 211.5 jit_solution(7609444026565786055)
XLA Ops:
  0.0 0.9 copy.49
  0.9 0.5 collective-permute-start
  1.4 0.7 reduce.6
  2.2 0.7 select_reduce_fusion
  3.3 0.7 copy.51
  3.9 7.9 %all-to-all-start = ((bf16[16,7,320]{2,1,0:T(8,128)(2,1)}), bf16[16,7,320]{2,1,0:T(8,128)(2,1)S(1)}, u32[]{:S(2)}, u32[]{:S(2)}) async-start(bf16[16,7,320]{2,1,0:T(8,128)(2,1)} %copy.51), calls=%async_computation | async-start | bytes 196608 | tf_op jit(solution)/shard_map/all_to_all | solution.py:201
  11.8 1.9 collective-permute-start.2
  13.9 0.8 dynamic_slice.28
  14.7 4.8 %all-to-all-done = bf16[16,7,320]{2,1,0:T(8,128)(2,1)S(1)} async-done(((bf16[16,7,320]{2,1,0:T(8,128)(2,1)}), bf16[16,7,320]{2,1,0:T(8,128)(2,1)S(1)}, u32[]{:S(2)}, u32[]{:S(2)}) %all-to-all-start) | async-done | bytes 71712 | tf_op jit(solution)/shard_map/all_to_all | solution.py:201
  19.6 0.3 convolution_convert_fusion
  19.9 0.9 reshape.224
  20.8 3.6 %all-to-all-start.1 = ((bf16[16,6,1536]{2,1,0:T(8,128)(2,1)}), bf16[16,6,1536]{2,1,0:T(8,128)(2,1)S(1)}, u32[]{:S(2)}, u32[]{:S(2)}) async-start(bf16[16,6,1536]{2,1,0:T(8,128)(2,1)} %reshape.224), calls=%async_computation.1 | async-start | bytes 786432 | tf_op jit(solution)/shard_map/all_to_all | solution.py:209
  24.4 1.0 dynamic-slice_bitcast_fusion
  25.6 37.4 %all-to-all-done.1 = bf16[16,6,1536]{2,1,0:T(8,128)(2,1)S(1)} async-done(((bf16[16,6,1536]{2,1,0:T(8,128)(2,1)}), bf16[16,6,1536]{2,1,0:T(8,128)(2,1)S(1)}, u32[]{:S(2)}, u32[]{:S(2)}) %all-to-all-start.1) | async-done | bytes 294944 | tf_op jit(solution)/shard_map/all_to_all | solution.py:209
  63.1 0.8 broadcast_in_dim.32
  63.9 5.3 %all-to-all-start.2 = ((bf16[16,6,1536]{2,1,0:T(8,128)(2,1)}), bf16[16,6,1536]{2,1,0:T(8,128)(2,1)S(1)}, u32[]{:S(2)}, u32[]{:S(2)}) async-start(bf16[16,6,1536]{2,1,0:T(8,128)(2,1)} %broadcast_in_dim.32), calls=%async_computation.2 | async-start | bytes 786432 | tf_op jit(solution)/shard_map/all_to_all | solution.py:213
  69.2 1.6 select_bitcast_fusion.7
  71.1 1.3 copy-done.7
  72.7 1.5 fusion.2
  74.2 2.4 %select_bitcast_fusion.5 = (bf16[1,320,1536]{2,1,0:T(8,128)(2,1)S(1)}, bf16[1,320,1536]{2,1,0:T(8,128)(2,1)}) fusion(bf16[320,1536]{1,0:T(8,128)(2,1)S(1)} %copy-done.8, bf16[320,1536]{1,0:T(8,128)(2,1)} %collective-permute-done.6, pred[]{:T(512)S(6)} %eq.48), kind=kLoop, calls=%fused_computation.28 | loop fusion | flops 983040 | bytes 3932161 | tf_op jit(solution)/shard_map/stack | solution.py:32
  76.5 4.5 %all-to-all-done.2 = bf16[16,6,1536]{2,1,0:T(8,128)(2,1)S(1)} async-done(((bf16[16,6,1536]{2,1,0:T(8,128)(2,1)}), bf16[16,6,1536]{2,1,0:T(8,128)(2,1)S(1)}, u32[]{:S(2)}, u32[]{:S(2)}) %all-to-all-start.2) | async-done | bytes 294944 | tf_op jit(solution)/shard_map/all_to_all | solution.py:213
  81.1 4.3 %all-to-all-start.3 = ((bf16[8,192,640]{2,1,0:T(8,128)(2,1)}), bf16[8,192,640]{2,1,0:T(8,128)(2,1)}, u32[]{:S(2)}, u32[]{:S(2)}) async-start(bf16[8,192,640]{2,1,0:T(8,128)(2,1)} %bitcast.104), calls=%async_computation.3 | async-start | bytes 3932160 | tf_op jit(solution)/shard_map/all_to_all | solution.py:182
  85.4 2.6 %pad_maximum_fusion.2 = bf16[2,320,1536]{2,1,0:T(8,128)(2,1)} fusion(bf16[1,320,1536]{2,1,0:T(8,128)(2,1)} %get-tuple-element.20, bf16[1,320,1536]{2,1,0:T(8,128)(2,1)S(1)} %get-tuple-element.19), kind=kLoop, calls=%fused_computation.15 | loop fusion | flops 983040 | bytes 3932160 | tf_op jit(solution)/shard_map/stack | solution.py:32
  88.1 0.8 dynamic_slice.29
  88.9 0.6 collective-permute-start.5
  90.2 3.5 %collective-permute-done.5 = bf16[96,320]{1,0:T(8,128)(2,1)S(1)} collective-permute-done((bf16[96,320]{1,0:T(8,128)(2,1)S(1)}, bf16[96,320]{1,0:T(8,128)(2,1)S(1)}, u32[]{:S(2)}, u32[]{:S(2)}) %collective-permute-start.5) | collective-permute-done | bytes 61472 | tf_op jit(solution)/shard_map/ppermute | solution.py:30
  93.9 0.8 reshape.232
  94.9 5.2 %select_bitcast_fusion.1 = (bf16[1,640,1536]{2,1,0:T(8,128)(2,1)}, bf16[1,640,1536]{2,1,0:T(8,128)(2,1)}, bf16[1,640,1536]{2,1,0:T(8,128)(2,1)S(1)}, bf16[1,640,1536]{2,1,0:T(8,128)(2,1)S(1)}) fusion(bf16[640,1536]{1,0:T(8,128)(2,1)} %collective-permute-done.7, pred[]{:T(512)S(6)} %eq.22, bf16[2,320,1536]{2,1,0:T(8,128)(2,1)} %pad_maximum_fusion.2, ...), kind=kLoop, calls=%fused_computation.17 | loop fusion | flops 3932160 | bytes 15728641 | tf_op jit(solution)/shard_map/stack | solution.py:32
  100.1 0.4 maximum_bitcast_fusion
  100.4 2.4 %copy.73 = bf16[2,80,8,1536]{3,2,0,1:T(8,128)(2,1)} copy(bf16[2,80,8,1536]{3,2,1,0:T(8,128)(2,1)S(1)} %maximum_bitcast_fusion) | data formatting | bytes 7864320 | tf_op jit(solution)/shard_map/reshape | solution.py:220
  102.9 4.5 %absorb.1.qk_ref = bf16[2304,640]{1,0:T(8,128)(2,1)S(1)} custom-call(bf16[96,3072]{1,0:T(8,128)(2,1)S(1)} %bitcast.98, bf16[640,3072]{1,0:T(8,128)(2,1)} %bitcast.102, f32[1,640]{1,0:T(1,128)S(1)} %reshape.229.gain_ref), custom_call_target="tpu_custom_call" | custom-call | tf_op jit(solution)/shard_map/absorb/pallas_call | solution.py:224
  107.5 1.6 copy-done.2
  109.0 20.2 %all-to-all-done.3 = bf16[8,192,640]{2,1,0:T(8,128)(2,1)} async-done(((bf16[8,192,640]{2,1,0:T(8,128)(2,1)}), bf16[8,192,640]{2,1,0:T(8,128)(2,1)}, u32[]{:S(2)}, u32[]{:S(2)}) %all-to-all-start.3) | async-done | bytes 1966112 | tf_op jit(solution)/shard_map/all_to_all | solution.py:182
  129.3 1.9 fusion.1
  131.2 0.5 copy-done.3
  131.7 10.6 %scores.1 = bf16[8,80,256]{2,1,0:T(8,128)(2,1)} custom-call(bf16[2304,640]{1,0:T(8,128)(2,1)S(1)} %copy-done.3, bf16[2048,640]{1,0:T(8,128)(2,1)S(1)} %bitcast.96, s32[8,1,256]{2,1,0:T(1,128)S(1)} %reshape.234.slot_ref), custom_call_target="tpu_custom_call" | custom-call | tf_op jit(solution)/shard_map/scores/pallas_call | solution.py:248
  142.3 3.4 %all-to-all-start.4 = ((bf16[8,80,256]{2,1,0:T(8,128)(2,1)}), bf16[8,80,256]{2,1,0:T(8,128)(2,1)S(1)}, u32[]{:S(2)}, u32[]{:S(2)}) async-start(bf16[8,80,256]{2,1,0:T(8,128)(2,1)} %scores.1), calls=%async_computation.4 | async-start | bytes 655360 | tf_op jit(solution)/shard_map/all_to_all | solution.py:261
  145.9 10.2 %all-to-all-done.4 = bf16[8,80,256]{2,1,0:T(8,128)(2,1)S(1)} async-done(((bf16[8,80,256]{2,1,0:T(8,128)(2,1)}), bf16[8,80,256]{2,1,0:T(8,128)(2,1)S(1)}, u32[]{:S(2)}, u32[]{:S(2)}) %all-to-all-start.4) | async-done | bytes 327712 | tf_op jit(solution)/shard_map/all_to_all | solution.py:261
  156.3 0.7 broadcast_in_dim.58
  157.1 3.6 %all-to-all-start.5 = ((bf16[8,80,256]{2,1,0:T(8,128)(2,1)}), bf16[8,80,256]{2,1,0:T(8,128)(2,1)S(1)}, u32[]{:S(2)}, u32[]{:S(2)}) async-start(bf16[8,80,256]{2,1,0:T(8,128)(2,1)} %broadcast_in_dim.58), calls=%async_computation.5 | async-start | bytes 655360 | tf_op jit(solution)/shard_map/all_to_all | solution.py:274
  160.8 2.5 %maximum_bitcast_fusion.1 = bf16[2,80,8,1536]{3,2,1,0:T(8,128)(2,1)S(1)} fusion(bf16[1,640,1536]{2,1,0:T(8,128)(2,1)} %get-tuple-element.14, bf16[1,640,1536]{2,1,0:T(8,128)(2,1)} %get-tuple-element.13), kind=kLoop, calls=%fused_computation.3 | loop fusion | flops 1966080 | bytes 7864320
  163.3 2.4 %copy.74 = bf16[2,80,8,1536]{3,2,0,1:T(8,128)(2,1)} copy(bf16[2,80,8,1536]{3,2,1,0:T(8,128)(2,1)S(1)} %maximum_bitcast_fusion.1) | data formatting | bytes 7864320 | tf_op jit(solution)/shard_map/reshape | solution.py:220
  165.8 5.2 %all-to-all-done.5.w_ref = bf16[8,80,256]{2,1,0:T(8,128)(2,1)S(1)} async-done(((bf16[8,80,256]{2,1,0:T(8,128)(2,1)}), bf16[8,80,256]{2,1,0:T(8,128)(2,1)S(1)}, u32[]{:S(2)}, u32[]{:S(2)}) %all-to-all-start.5) | async-done | bytes 327712 | tf_op jit(solution)/shard_map/all_to_all | solution.py:274
  170.9 13.7 %values.1 = (bf16[96,3072]{1,0:T(8,128)(2,1)S(1)}, f32[72,32]{1,0:T(8,128)S(1)}) custom-call(bf16[8,80,256]{2,1,0:T(8,128)(2,1)S(1)} %all-to-all-done.5.w_ref, bf16[2048,640]{1,0:T(8,128)(2,1)S(1)} %bitcast.97, s32[1,2048]{1,0:T(1,128)S(1)} %bitcast.100, bf16[640,3072]{1,0:T(8,128)(2,1)} %bitcast.101, f32[1,640]{1,0:T(1,128)S(1)} %reshape.229.gain_ref), custom_call_target="tpu_custom_call" | custom-call | tf_op jit(solution)/shard_map/values/pallas_call | solution.py:279
  184.6 0.6 copy-done.4
  185.2 0.4 reshape.238
  186.8 23.1 %all_to_all.35 = bf16[32,8,1536]{2,1,0:T(8,128)(2,1)S(1)} all-to-all(bf16[32,8,1536]{2,1,0:T(8,128)(2,1)S(1)} %bitcast.105), channel_id=1, replica_groups=mesh['seq'=16,'tp'=2] {'seq','tp'}, dimensions={0} | all-to-all | bytes 1572864 | tf_op jit(solution)/shard_map/all_to_all | solution.py:300
  210.9 0.6 copy.65
  (99 shorter events, 5.0 us)
Async XLA Ops:
  0.0 19.6 %copy-start = (bf16[320,1536]{1,0:T(8,128)(2,1)S(1)}, bf16[320,1536]{1,0:T(8,128)(2,1)}, u32[]{:S(2)}) copy-start(bf16[320,1536]{1,0:T(8,128)(2,1)} %param.17) | copy-start | bytes 2949124
  0.9 2.1 collective-permute-start
  3.0 21.3 %copy-start.6 = (bf16[384,2560]{1,0:T(8,128)(2,1)S(1)}, bf16[384,2560]{1,0:T(8,128)(2,1)}, u32[]{:S(2)}) copy-start(bf16[384,2560]{1,0:T(8,128)(2,1)} %param.9) | copy-start | bytes 5898244
  3.9 15.6 %all-to-all-start = ((bf16[16,7,320]{2,1,0:T(8,128)(2,1)}), bf16[16,7,320]{2,1,0:T(8,128)(2,1)S(1)}, u32[]{:S(2)}, u32[]{:S(2)}) async-start(bf16[16,7,320]{2,1,0:T(8,128)(2,1)} %copy.51), calls=%async_computation | async-start | bytes 196608 | tf_op jit(solution)/shard_map/all_to_all | solution.py:201
  11.8 57.3 %collective-permute-start.2 = (bf16[320,1536]{1,0:T(8,128)(2,1)}, bf16[320,1536]{1,0:T(8,128)(2,1)}, u32[]{:S(2)}, u32[]{:S(2)}) collective-permute-start(bf16[320,1536]{1,0:T(8,128)(2,1)} %param.15), channel_id=1, source_target_pairs={{0,2},{2,0},{4,6},{6,4},{8,10},{10,8},{12,14},{14,12},{16,18},{18,... | collective-permute-start | bytes 2949128 | tf_op jit(solution)/shard_map/ppermute | solution.py:30
  13.8 60.4 %collective-permute-start.6 = (bf16[320,1536]{1,0:T(8,128)(2,1)}, bf16[320,1536]{1,0:T(8,128)(2,1)}, u32[]{:S(2)}, u32[]{:S(2)}) collective-permute-start(bf16[320,1536]{1,0:T(8,128)(2,1)} %param.16), channel_id=1, source_target_pairs={{0,2},{2,0},{4,6},{6,4},{8,10},{10,8},{12,14},{14,12},{16,18},{18,... | collective-permute-start | bytes 2949128 | tf_op jit(solution)/shard_map/ppermute | solution.py:30
  20.8 42.1 %all-to-all-start.1 = ((bf16[16,6,1536]{2,1,0:T(8,128)(2,1)}), bf16[16,6,1536]{2,1,0:T(8,128)(2,1)S(1)}, u32[]{:S(2)}, u32[]{:S(2)}) async-start(bf16[16,6,1536]{2,1,0:T(8,128)(2,1)} %reshape.224), calls=%async_computation.1 | async-start | bytes 786432 | tf_op jit(solution)/shard_map/all_to_all | solution.py:209
  25.4 45.7 %collective-permute-start.4 = (bf16[192,2560]{1,0:T(8,128)(2,1)}, bf16[192,2560]{1,0:T(8,128)(2,1)S(1)}, u32[]{:S(2)}, u32[]{:S(2)}) collective-permute-start(bf16[192,2560]{1,0:T(8,128)(2,1)} %dynamic-slice_bitcast_fusion), channel_id=1, source_target_pairs={{0,1},{1,0},{2,3},{3,2},{4,5},{5,4},{6,7},{7,6},{8,9},{9,8},{10,11... | collective-permute-start | bytes 2949128 | tf_op jit(solution)/shard_map/ppermute | solution.py:175
  63.9 17.2 %all-to-all-start.2 = ((bf16[16,6,1536]{2,1,0:T(8,128)(2,1)}), bf16[16,6,1536]{2,1,0:T(8,128)(2,1)S(1)}, u32[]{:S(2)}, u32[]{:S(2)}) async-start(bf16[16,6,1536]{2,1,0:T(8,128)(2,1)} %broadcast_in_dim.32), calls=%async_computation.2 | async-start | bytes 786432 | tf_op jit(solution)/shard_map/all_to_all | solution.py:213
  70.8 1.5 copy-start.7
  71.0 23.9 %collective-permute-start.3 = (bf16[640,1536]{1,0:T(8,128)(2,1)S(1)}, bf16[640,1536]{1,0:T(8,128)(2,1)}, u32[]{:S(2)}, u32[]{:S(2)}) collective-permute-start(bf16[640,1536]{1,0:T(8,128)(2,1)S(1)} %bitcast.103), channel_id=1, source_target_pairs={{0,1},{1,0},{2,3},{3,2},{4,5},{5,4},{6,7},{7,6},{8,9},{9,8},{10,11... | collective-permute-start | bytes 5898248 | tf_op jit(solution)/shard_map/ppermute | solution.py:30
  72.7 1.5 copy-start.8
  81.1 48.2 %all-to-all-start.3 = ((bf16[8,192,640]{2,1,0:T(8,128)(2,1)}), bf16[8,192,640]{2,1,0:T(8,128)(2,1)}, u32[]{:S(2)}, u32[]{:S(2)}) async-start(bf16[8,192,640]{2,1,0:T(8,128)(2,1)} %bitcast.104), calls=%async_computation.3 | async-start | bytes 3932160 | tf_op jit(solution)/shard_map/all_to_all | solution.py:182
  88.1 6.8 %collective-permute-start.7 = (bf16[640,1536]{1,0:T(8,128)(2,1)}, bf16[640,1536]{1,0:T(8,128)(2,1)}, u32[]{:S(2)}, u32[]{:S(2)}) collective-permute-start(bf16[640,1536]{1,0:T(8,128)(2,1)} %bitcast.28), channel_id=1, source_target_pairs={{0,1},{1,0},{2,3},{3,2},{4,5},{5,4},{6,7},{7,6},{8,9},{9,8},{10,11... | collective-permute-start | bytes 5898248 | tf_op jit(solution)/shard_map/ppermute | solution.py:30
  88.9 4.7 %collective-permute-start.5 = (bf16[96,320]{1,0:T(8,128)(2,1)S(1)}, bf16[96,320]{1,0:T(8,128)(2,1)S(1)}, u32[]{:S(2)}, u32[]{:S(2)}) collective-permute-start(bf16[96,320]{1,0:T(8,128)(2,1)S(1)} %reshape.223), channel_id=1, source_target_pairs={{0,2},{2,0},{4,6},{6,4},{8,10},{10,8},{12,14},{14,12},{16,18},{18,... | collective-permute-start | bytes 184328 | tf_op jit(solution)/shard_map/ppermute | solution.py:30
  89.9 4.8 %collective-permute-start.1 = (bf16[96,1536]{1,0:T(8,128)(2,1)S(1)}, bf16[96,1536]{1,0:T(8,128)(2,1)S(1)}, u32[]{:S(2)}, u32[]{:S(2)}) collective-permute-start(bf16[96,1536]{1,0:T(8,128)(2,1)S(1)} %reshape.225), channel_id=1, source_target_pairs={{0,1},{1,0},{2,3},{3,2},{4,5},{5,4},{6,7},{7,6},{8,9},{9,8},{10,11... | collective-permute-start | bytes 884744 | tf_op jit(solution)/shard_map/ppermute | solution.py:30
  102.9 26.4 %copy-start.9 = (bf16[8,12,640]{2,1,0:T(8,128)(2,1)S(1)}, bf16[8,12,640]{2,1,0:T(8,128)(2,1)}, u32[]{:S(2)}) copy-start(bf16[8,12,640]{2,1,0:T(8,128)(2,1)} %reshape.232) | copy-start | bytes 368644
  107.4 1.6 copy-start.2
  129.3 2.4 %copy-start.3 = (bf16[2304,640]{1,0:T(8,128)(2,1)S(1)}, bf16[2304,640]{1,0:T(8,128)(2,1)}, u32[]{:S(2)}) copy-start(bf16[2304,640]{1,0:T(8,128)(2,1)} %copy-done.2) | copy-start | bytes 8847364
  142.3 13.8 %all-to-all-start.4 = ((bf16[8,80,256]{2,1,0:T(8,128)(2,1)}), bf16[8,80,256]{2,1,0:T(8,128)(2,1)S(1)}, u32[]{:S(2)}, u32[]{:S(2)}) async-start(bf16[8,80,256]{2,1,0:T(8,128)(2,1)} %scores.1), calls=%async_computation.4 | async-start | bytes 655360 | tf_op jit(solution)/shard_map/all_to_all | solution.py:261
  157.1 13.8 %all-to-all-start.5 = ((bf16[8,80,256]{2,1,0:T(8,128)(2,1)}), bf16[8,80,256]{2,1,0:T(8,128)(2,1)S(1)}, u32[]{:S(2)}, u32[]{:S(2)}) async-start(bf16[8,80,256]{2,1,0:T(8,128)(2,1)} %broadcast_in_dim.58), calls=%async_computation.5 | async-start | bytes 655360 | tf_op jit(solution)/shard_map/all_to_all | solution.py:274
  184.6 0.6 copy-start.4
  185.2 0.8 copy-start.5
  209.9 1.6 copy-start.1

commit v2 on v1

v2 whole, which is shorter than its diff:
```python
import functools
import math

import jax
import jax.numpy as jnp
from jax import lax
from jax.experimental import pallas as pl
from jax.experimental.pallas import tpu as pltpu
from jax.sharding import PartitionSpec as P

HEAD = 128
PAIR = 2
SLOTS = 4
BLOCKS = 4
NT = (((1,), (1,)), ((), ()))
VMEM_LIMIT = 48 * 1024 * 1024


def params():
    return pltpu.CompilerParams(vmem_limit_bytes=VMEM_LIMIT)


def split(values):
    high = values.astype(jnp.bfloat16)
    return high, (values - high.astype(jnp.float32)).astype(jnp.bfloat16)


def halves(values):
    high = lax.reduce_precision(values, 8, 7)
    return high.astype(jnp.bfloat16), (values - high).astype(jnp.bfloat16)


def thirds(values):
    high = lax.reduce_precision(values, 8, 7)
    return high.astype(jnp.bfloat16), *halves(values - high)


def swap_gather(values, axis, size, index, perm):
    if size == 1:
        return values[None]
    other = lax.ppermute(values, axis, perm)
    first = index == 0
    return jnp.stack([jnp.where(first, values, other), jnp.where(first, other, values)])


def put_lanes(ref, rows, values):
    for tile in range(ref.shape[0]):
        part = values[:, tile * 128 : (tile + 1) * 128]
        if part.shape[1] < 128:
            fill = jnp.zeros((part.shape[0], 128 - part.shape[1]), part.dtype)
            part = jnp.concatenate([part, fill], axis=1)
        ref[tile, rows, :] = part


def take_lanes(ref, rows, width):
    tiles = [ref[tile, rows, :] for tile in range(ref.shape[0])]
    return jnp.concatenate(tiles, axis=1)[:, :width]


def absorb_kernel(count, *refs):
    queries, weights = refs[:count], refs[count : 2 * count]
    gain_ref, out_ref, rows_ref = refs[2 * count :]
    rows, per = queries[0].shape[0], queries[0].shape[1] // HEAD
    gain = gain_ref[...]
    for piece in range(count):
        for head in range(per):
            lanes = pl.ds(head * HEAD, HEAD)
            mixed = lax.dot_general(
                queries[piece][:, lanes], weights[piece][:, lanes], NT,
                preferred_element_type=jnp.float32,
            )
            place = pl.ds(piece * per + head, rows, stride=count * per)
            put_lanes(rows_ref, place, mixed * gain)
    out_ref[...] = take_lanes(rows_ref, slice(None), out_ref.shape[1]).astype(jnp.bfloat16)


def score_tile(slots, per_slot, qk_ref, x, slot):
    tokens = x.shape[0]
    slot = jnp.broadcast_to(slot, (per_slot, tokens))
    depth = SLOTS * per_slot
    scores = jnp.zeros((per_slot, tokens), jnp.float32)
    for group in range(slots // SLOTS):
        part = lax.dot_general(
            qk_ref[group * depth : (group + 1) * depth, :], x, NT,
            preferred_element_type=jnp.float32,
        )
        for j in range(SLOTS):
            here = slot == group * SLOTS + j
            scores = jnp.where(here, part[j * per_slot : (j + 1) * per_slot], scores)
    values = x.astype(jnp.float32)
    high, low = split(values * values)
    ones = jnp.ones((8, x.shape[1]), jnp.bfloat16)
    total = lax.dot_general(ones, high, NT, preferred_element_type=jnp.float32)
    total = total + lax.dot_general(ones, low, NT, preferred_element_type=jnp.float32)
    total_high, total_low = split(total)
    row = lax.broadcasted_iota(jnp.int32, total.shape, 0)
    total = jnp.where(
        row == 0, total_high.astype(jnp.float32), jnp.where(row == 1, total_low.astype(jnp.float32), 0.0)
    )
    return jnp.concatenate([scores, total], axis=0).astype(jnp.bfloat16)


def score_kernel(
    slots, per_slot, new_cols, qk_ref, slot_ref, new_slot_ref, slab_ref, new_ref, out_ref
):
    shards, own, wide = slab_ref.shape
    new = score_tile(slots, per_slot, qk_ref, new_ref[...], new_slot_ref[...])
    batch = BLOCKS if shards % BLOCKS == 0 else 1
    for first in range(0, shards, batch):
        x = slab_ref[first : first + batch].reshape(batch * own, wide)
        slot = slot_ref[:, first * own : (first + batch) * own]
        tile = score_tile(slots, per_slot, qk_ref, x, slot)
        for i in range(batch):
            out_ref[first + i, :, 0:own] = tile[:, i * own : (i + 1) * own]
    for place in range(shards):
        out_ref[place, :, own : own + new_cols] = new[:, place * new_cols : (place + 1) * new_cols]
        rest = out_ref.shape[2] - own - new_cols
        out_ref[place, :, own + new_cols :] = jnp.zeros((per_slot + 8, rest), jnp.bfloat16)


def value_kernel(
    slots, per_slot, new_cols, count, w_ref, slot_ref, gain_ref, slab_ref, new_ref, *refs
):
    weights_in, outs = refs[:count], refs[count : 2 * count]
    d_ref, x_ref, w_all, p_ref, mixed_ref = refs[2 * count :]
    shards, own, _ = slab_ref.shape
    tokens = w_all.shape[1]
    w_all[:, shards * own :] = jnp.zeros((per_slot + 8, tokens - shards * own), jnp.bfloat16)
    for b in range(shards):
        x_ref[b * own : (b + 1) * own, :] = slab_ref[b]
        w_all[:, b * own : (b + 1) * own] = w_ref[b, :, 0:own]
        start = shards * own + b * new_cols
        w_all[:, start : start + new_cols] = w_ref[b, :, own : own + new_cols]
    x_ref[shards * own :, :] = new_ref[...]
    slot = slot_ref[...]
    one_hot = (
        lax.broadcasted_iota(jnp.int32, (slots, tokens), 0) == slot
    ).astype(jnp.float32).astype(jnp.bfloat16)
    weights = w_all[:per_slot, :]
    total = lax.dot_general(weights, one_hot, NT, preferred_element_type=jnp.float32)
    by_slot = lax.dot_general(one_hot, weights, NT, preferred_element_type=jnp.float32)
    steps = d_ref.shape[0] // slots
    heads = per_slot // steps
    fill = jnp.zeros((slots, 128 - heads), jnp.float32)
    for step_id in range(steps):
        part = by_slot[:, step_id * heads : (step_id + 1) * heads]
        d_ref[pl.ds(step_id, slots, stride=steps), :] = jnp.concatenate([part, fill], axis=1)
    inverse = jnp.where(total > 0.0, 1.0 / jnp.where(total > 0.0, total, 1.0), 0.0)
    high, low = split(inverse)
    scale = jnp.dot(high, one_hot, preferred_element_type=jnp.float32)
    scale = scale + jnp.dot(low, one_hot, preferred_element_type=jnp.float32)
    extra = w_all[per_slot:, :].astype(jnp.float32)
    factor = extra[0:1] + extra[1:2]
    p_ref[...] = weights.astype(jnp.float32) * scale * factor
    depth = SLOTS * per_slot
    gain = gain_ref[...]

    def step(group, carry):
        p = p_ref[...]
        wide = jnp.broadcast_to(slot, p.shape)
        rows = [jnp.where(wide == group * SLOTS + j, p, 0.0) for j in range(SLOTS)]
        mixed = jnp.dot(
            jnp.concatenate(rows, axis=0).astype(jnp.bfloat16), x_ref[...],
            preferred_element_type=jnp.float32,
        )
        put_lanes(mixed_ref, pl.ds(pl.multiple_of(group * depth, depth), depth), mixed * gain)
        return carry

    lax.fori_loop(0, slots // SLOTS, step, 0, unroll=2)
    rows, per = outs[0].shape[0], outs[0].shape[1] // HEAD
    for piece in range(count):
        for head in range(per):
            place = pl.ds(piece * per + head, rows, stride=count * per)
            mixed = take_lanes(mixed_ref, place, x_ref.shape[1]).astype(jnp.bfloat16)
            lanes = pl.ds(head * HEAD, HEAD)
            outs[piece][:, lanes] = jnp.dot(
                mixed, weights_in[piece][:, lanes], preferred_element_type=jnp.float32
            ).astype(jnp.bfloat16)


def join_kernel(own_rows, part_ref, theirs_ref, d_ref, theirs_d_ref, out_ref):
    rows, width = part_ref.shape
    heads = width // HEAD
    mine, theirs = d_ref[:, :heads], theirs_d_ref[:, heads : 2 * heads]
    joined = mine + theirs
    inverse = jnp.where(joined > 0.0, 1.0 / jnp.where(joined > 0.0, joined, 1.0), 0.0)
    mine, theirs = mine * inverse, theirs * inverse
    joined = jnp.concatenate([joined, jnp.zeros((rows, 128 - heads), jnp.float32)], axis=1)
    high, low = split(joined)
    high, low = high.astype(jnp.float32), low.astype(jnp.float32)
    for head in range(heads):
        lanes = pl.ds(head * HEAD, HEAD)
        value = part_ref[:, lanes].astype(jnp.float32) * mine[:, head : head + 1]
        value = value + theirs_ref[:, lanes].astype(jnp.float32) * theirs[:, head : head + 1]
        for i in range(rows // own_rows):
            if head < own_rows:
                row = slice(i * own_rows + head, i * own_rows + head + 1)
                extra = [high[row], low[row]]
            else:
                extra = [jnp.zeros((2, HEAD), jnp.float32)]
            block = jnp.concatenate([value[i * own_rows : (i + 1) * own_rows]] + extra, axis=0)
            out_ref[i, :, lanes] = block.astype(jnp.bfloat16)


def on_device(
    slab, token_request, request_slot, new_states, cache_gain, query_gain,
    key_weight, value_weight, query_weight,
):
    f32, bf16 = jnp.float32, jnp.bfloat16
    seq, tp = lax.axis_size("seq"), lax.axis_size("tp")
    k, c = lax.axis_index("seq"), lax.axis_index("tp")
    tokens, half = slab.shape
    model = half * tp
    own = tokens // tp
    feat = model // seq
    pair = PAIR if seq % PAIR == 0 else 1
    shards = seq // pair
    wide = feat * pair
    x, m = k % pair, k // pair
    groups = [[pair * i + p for i in range(shards)] for p in range(pair)]
    x_perm = [(i, i ^ 1) for i in range(seq)]
    tp_perm = [(0, 1), (1, 0)]
    local_width = key_weight.shape[1]
    heads_local = local_width // HEAD
    heads = heads_local * tp
    per, steps, _ = new_states.shape
    slots = request_slot.shape[0]
    own_rows = per * steps
    rows = slots * steps
    per_slot = steps * heads
    scale = 1.0 / math.sqrt(HEAD)

    def over_tp(values):
        if tp == 2:
            return [values, lax.ppermute(values, "tp", tp_perm)]
        everyone = lax.all_gather(values, "tp", axis=0, tiled=False)
        return [everyone[i] for i in range(tp)]

    cut = slab.reshape(tp, own, half)
    if tp == 2:
        mine = lax.dynamic_index_in_dim(cut, c, 0, keepdims=False)
        other = lax.ppermute(
            lax.dynamic_index_in_dim(cut, 1 - c, 0, keepdims=False), "tp", tp_perm
        )
        whole = jnp.stack([jnp.where(c == 0, mine, other), jnp.where(c == 0, other, mine)])
    else:
        whole = lax.all_to_all(cut, "tp", 0, 0, tiled=True)
    message = whole.reshape(tp, own, shards // tp, wide).transpose(0, 2, 1, 3)
    message = message.reshape(shards, own, wide)

    requests = lax.dynamic_index_in_dim(token_request.reshape(tp, own), c, 0, keepdims=False)
    match = requests[None, :] == jnp.arange(slots, dtype=jnp.int32)[:, None]
    target = jnp.sum(jnp.where(match, request_slot[:, None], 0), axis=0)
    states = over_tp(new_states.reshape(own_rows, half))
    if tp == 2:
        states = [jnp.where(c == 0, states[i], states[1 - i]) for i in range(2)]
    states = jnp.concatenate(states, axis=1)
    squares = states.astype(f32)
    own_factor = lax.rsqrt(jnp.mean(squares * squares, axis=-1, keepdims=True) + 1e-06)
    carried = jnp.concatenate([target.astype(bf16), *thirds(own_factor[:, 0])])
    carried_rows = -(-carried.shape[0] // feat)
    carried = jnp.pad(carried, (0, carried_rows * feat - carried.shape[0]))
    carried = jnp.broadcast_to(carried.reshape(1, carried_rows, feat), (seq, carried_rows, feat))
    sent = jnp.concatenate(
        [states.reshape(own_rows, seq, feat).transpose(1, 0, 2), carried], axis=1
    )
    got = lax.all_to_all(sent, "seq", 0, 0, tiled=True)
    state_part = got[:, :own_rows].reshape(rows, feat)
    carried = got[:, own_rows:].reshape(seq, carried_rows * feat)
    slots_in = carried[:, :own].reshape(shards, pair, own)
    slots_in = lax.dynamic_index_in_dim(slots_in, x, 1, keepdims=False).astype(jnp.int32)
    row_factor = carried[:, own : own + 3 * own_rows].astype(f32).reshape(seq, 3, own_rows)
    row_factor = (row_factor[:, 0] + row_factor[:, 1] + row_factor[:, 2]).reshape(rows, 1)

    exchange = functools.partial(
        lax.all_to_all, axis_name="seq", split_axis=0, concat_axis=0, tiled=True,
        axis_index_groups=groups,
    )
    gain_part = lax.dynamic_slice(query_gain, (k * feat,), (feat,))
    query_part = (state_part.astype(f32) * row_factor * gain_part).astype(bf16)
    partial = jnp.dot(query_part, query_weight, preferred_element_type=f32)
    partial = partial.reshape(seq, own_rows, local_width)
    partial = partial.astype(bf16)
    partial = lax.all_to_all(partial, "seq", 0, 0, tiled=True)
    query = jnp.sum(partial.astype(f32), axis=0).astype(bf16)
    queries = lax.all_to_all(
        jnp.broadcast_to(query[None], (seq, own_rows, local_width)), "seq", 0, 0, tiled=True
    ).reshape(rows, local_width)
    state_wide = swap_gather(state_part, "seq", pair, x, x_perm)
    queries, state_wide, message, key_weight, value_weight = lax.optimization_barrier(
        (queries, state_wide, message, key_weight, value_weight)
    )
    slab_in = exchange(message)
    queries = over_tp(queries)

    def join_pair(first, second):
        if pair == 1:
            return first
        low = x == 0
        return jnp.concatenate(
            [jnp.where(low, first, second), jnp.where(low, second, first)], axis=0
        )

    def from_pair(values):
        return values if pair == 1 else lax.ppermute(values, "seq", x_perm)

    keys_full = over_tp(join_pair(key_weight, from_pair(key_weight)))
    value_other = from_pair(value_weight)
    gain = lax.dynamic_slice(cache_gain, (m * wide,), (wide,)).reshape(1, wide)
    absorbed = pl.pallas_call(
        functools.partial(absorb_kernel, tp),
        out_shape=jax.ShapeDtypeStruct((rows * heads, wide), bf16),
        scratch_shapes=[pltpu.VMEM((-(-wide // 128), rows * heads, 128), f32)],
        compiler_params=params(),
        name="absorb",
    )(*queries, *keys_full, gain)

    new_cols = rows // shards
    width = -(-(own + new_cols) // 128) * 128
    new_width = -(-rows // 128) * 128
    state_wide = state_wide.transpose(1, 0, 2).reshape(rows, wide)
    state_wide = jnp.pad(state_wide, ((0, new_width - rows), (0, 0)))
    group = x * tp + c
    new_slot = jnp.arange(rows, dtype=jnp.int32) // steps
    new_slot = jnp.where(new_slot % (pair * tp) == group, new_slot, -1)
    slot_row = slots_in.reshape(1, shards * own)
    new_row = jnp.pad(new_slot, (0, new_width - rows), constant_values=-1)[None]
    out_rows = per_slot + 8
    partial = pl.pallas_call(
        functools.partial(score_kernel, slots, per_slot, new_cols),
        out_shape=jax.ShapeDtypeStruct((shards, out_rows, width), bf16),
        compiler_params=params(),
        name="scores",
    )(absorbed, slot_row, new_row, slab_in, state_wide)
    partial, value_other = lax.optimization_barrier((partial, value_other))
    partial = lax.all_to_all(partial, "seq", 0, 0, tiled=True, axis_index_groups=groups)
    values_full = over_tp(join_pair(value_weight, value_other))
    summed = jnp.sum(partial.astype(f32), axis=0)
    mean = (summed[per_slot] + summed[per_slot + 1]) / model
    factor = lax.rsqrt(mean + 1e-06)[None]
    my_new = lax.dynamic_slice(new_slot, (m * new_cols,), (new_cols,))
    spare = jnp.full((width - own - new_cols,), -1, jnp.int32)
    my_slot = jnp.concatenate([target, my_new, spare])[None]
    column = jnp.arange(width, dtype=jnp.int32)[None]
    step_of = jnp.arange(per_slot, dtype=jnp.int32)[:, None] // heads
    seen = (my_slot >= 0) & ((column < own) | ((column - own) % steps <= step_of))
    weights = jnp.where(seen, jnp.exp(summed[:per_slot] * (factor * scale)), 0.0)
    high, low = halves(factor)
    ready = jnp.concatenate(
        [weights.astype(bf16), high, low, jnp.zeros((6, width), bf16)], axis=0
    )
    weights_in = lax.all_to_all(
        jnp.broadcast_to(ready[None], (shards, out_rows, width)),
        "seq", 0, 0, tiled=True, axis_index_groups=groups,
    )

    tokens_all = shards * own + new_width
    *attended, totals = pl.pallas_call(
        functools.partial(value_kernel, slots, per_slot, new_cols, tp),
        out_shape=tuple(
            jax.ShapeDtypeStruct((rows, local_width), bf16) for _ in range(tp)
        ) + (jax.ShapeDtypeStruct((rows, 128), f32),),
        scratch_shapes=[
            pltpu.VMEM((tokens_all, wide), bf16),
            pltpu.VMEM((out_rows, tokens_all), bf16),
            pltpu.VMEM((per_slot, tokens_all), f32),
            pltpu.VMEM((-(-wide // 128), rows * heads, 128), f32),
        ],
        compiler_params=params(),
        name="values",
    )(
        weights_in, jnp.concatenate([slot_row, new_row], axis=1), gain, slab_in, state_wide,
        *values_full,
    )

    if tp == 2 and own_rows <= heads_local:
        sent = pl.pallas_call(
            functools.partial(join_kernel, own_rows),
            out_shape=jax.ShapeDtypeStruct((seq, own_rows + 2, local_width), bf16),
            compiler_params=params(),
            name="join",
        )(
            attended[0], lax.ppermute(attended[1], "tp", tp_perm),
            totals, lax.ppermute(totals, "tp", tp_perm),
        )
        axes, groups_in, stride = "seq", pair, HEAD
    else:
        parts = jnp.stack([part.reshape(seq, own_rows, local_width) for part in attended], axis=1)
        totals = totals[:, :heads].reshape(seq, own_rows, tp, heads_local).transpose(0, 2, 1, 3)
        totals = jnp.stack(halves(totals), axis=2).reshape(seq, tp, 2, own_rows * heads_local)
        spare = local_width - own_rows * heads_local
        totals = jnp.pad(totals, ((0, 0), (0, 0), (0, 0), (0, spare)))
        sent = jnp.concatenate([parts, totals], axis=2)
        sent = sent.reshape(seq * tp, own_rows + 2, local_width)
        axes, groups_in, stride = ("seq", "tp"), pair * tp, heads_local
    got = lax.all_to_all(sent, axes, 0, 0, tiled=True)
    got = got.reshape(shards, groups_in, own_rows + 2, local_width).astype(f32)
    sums = jnp.sum(got[:, :, :own_rows], axis=0)
    share = got[0, :, own_rows, :] + got[0, :, own_rows + 1, :]
    share = share[:, : own_rows * stride].reshape(groups_in, own_rows, stride)[..., :heads_local]
    share = share / jnp.sum(share, axis=0, keepdims=True)
    sums = sums.reshape(groups_in, own_rows, heads_local, HEAD) * share[..., None]
    return jnp.sum(sums, axis=0).reshape(per, steps, local_width).astype(bf16)


def solution(mesh):
    placed = (
        P("seq", "tp"),
        P("seq", None),
        P(),
        P("seq", None, "tp"),
        P(),
        P(),
        P("seq", "tp"),
        P("seq", "tp"),
        P("seq", "tp"),
    )
    return jax.shard_map(
        on_device, mesh=mesh, in_specs=placed, out_specs=P("seq", None, "tp"), check_vma=False
    )
```

time: 213 us -> 178 us (0.84)
  waiting for transfers between devices: 85.9 us -> 68.2 us
  blocking collectives: 23.1 us -> 17 us
  other arithmetic: 21.9 us -> 16.8 us
  local copies, waits for them, and re-layouts: 19.3 us -> 15 us
  Pallas kernels: 28.8 us -> 26.6 us
    all_to_all x2, waiting for transfers between devices: 57.6 us -> 18.7 us  [the longest x1 13.4 us: on_device(): slab_in = exchange(message)]
    ppermute x0 -> x8, waiting for transfers between devices: none -> 16.4 us  [the longest x2 15.3 us: from_pair(): return values if pair == 1 else lax.ppermute(values, 'seq', x_perm)]
    another operation x8 -> x2, other arithmetic: 12.1 us -> 1.61 us  [swap_gather(): jnp.stack([jnp.where(first, values, other), jnp.where(first, other, value...]
    all_to_all x1, blocking collectives: 23.1 us -> 17 us  [on_device(): got = lax.all_to_all(sent, axes, 0, 0, tiled=True)]
    reshape x12 -> x8, local copies, waits for them, and re-layouts: 7.39 us -> 2.01 us  [the longest x1 1.72 us: on_device(): state_wide = state_wide.transpose(1, 0, 2).reshape(rows, wide)]
    all_to_all x1, waiting for transfers between devices: 5.18 us -> 10.2 us  [on_device(): lax.all_to_all(jnp.broadcast_to(ready[None], (shards, out_rows, width)),...]
    select_n x1 -> x4, other arithmetic: 0.02 us -> 4.55 us  [the longest x2 4.52 us: join_pair(): jnp.where(low, first, second)]
    all_to_all x1, waiting for transfers between devices: 4.54 us -> 8.07 us  [on_device(): lax.all_to_all(jnp.broadcast_to(query[None], (seq, own_rows, local_width)...]
  transfers between devices with their start and end apart: 14 -> 16, of which waited for: 7 -> 9; matrix products, arithmetic and copies ran while one was open for 14% -> 13% of each run, Pallas kernels for 2% -> 8%
where the time goes in v2:
time: 178 us; the launch traced here: 176 us
  waiting for transfers between devices  68.2 us (38%)
  starting transfers between devices  32.1 us (18%)
  Pallas kernels  26.6 us (15%)
  blocking collectives  17 us (10%)
  other arithmetic  16.8 us (9%)
  local copies, waits for them, and re-layouts  15 us (8%)
    all_to_all x1, blocking collectives, on_device(): got = lax.all_to_all(sent, axes, 0, 0, tiled=True)  17 us
    ppermute x2, waiting for transfers between devices, from_pair(): return values if pair == 1 else lax.ppermute(values, 'seq', x_perm)  15.3 us
    all_to_all x1, waiting for transfers between devices, on_device(): slab_in = exchange(message)  13.4 us
    pallas_call x1, Pallas kernels, on_device(): pl.pallas_call(functools.partial(value_kernel, slots, per_slot, new_cols,...  11.5 us
    all_to_all x1, waiting for transfers between devices, on_device(): lax.all_to_all(jnp.broadcast_to(ready[None], (shards, out_rows, width)),...  10.2 us
    pallas_call x1, Pallas kernels, on_device(): pl.pallas_call(functools.partial(score_kernel, slots, per_slot, new_cols)...  8.34 us
    all_to_all x1, waiting for transfers between devices, on_device(): lax.all_to_all(jnp.broadcast_to(query[None], (seq, own_rows, local_width)...  8.07 us
    all_to_all x1, starting transfers between devices, on_device(): got = lax.all_to_all(sent, 'seq', 0, 0, tiled=True)  7.88 us
  transfers between devices with their start and end apart: 16, of which 9 were waited for; matrix products, arithmetic and copies ran while one was open for 13% of the time, Pallas kernels for 8%

profile of v2, /device:TPU:0, one launch (start us, length us, event | category | flops | bytes accessed | tf_op | source)
XLA Modules:
  0.0 176.4 jit_solution(12662551399672818991)
XLA Ops:
  0.0 0.9 copy.47
  0.9 0.5 collective-permute-start
  1.4 0.7 reduce.5
  2.2 0.7 select_reduce_fusion
  3.5 0.7 pad_maximum_fusion.4
  4.1 7.9 %all-to-all-start = ((bf16[16,7,320]{2,1,0:T(8,128)(2,1)}), bf16[16,7,320]{2,1,0:T(8,128)(2,1)S(1)}, u32[]{:S(2)}, u32[]{:S(2)}) async-start(bf16[16,7,320]{2,1,0:T(8,128)(2,1)} %pad_maximum_fusion.4), calls=%async_computation | async-start | bytes 196608 | tf_op jit(solution)/shard_map/all_to_all | solution.py:267
  12.0 2.2 %dynamic-slice_bitcast_fusion = bf16[192,2560]{1,0:T(8,128)(2,1)} fusion(bf16[2,192,2560]{2,1,0:T(8,128)(2,1)} %bitcast.48, s32[]{:T(128)S(6)} %select_n.153), kind=kLoop, calls=%fused_computation.16 | loop fusion | bytes 1966084 | tf_op jit(solution)/shard_map/jit(dynamic_index_in_dim)/squeeze | solution.py:243
  14.5 0.8 dynamic_slice.26
  15.2 4.5 %all-to-all-done = bf16[16,7,320]{2,1,0:T(8,128)(2,1)S(1)} async-done(((bf16[16,7,320]{2,1,0:T(8,128)(2,1)}), bf16[16,7,320]{2,1,0:T(8,128)(2,1)S(1)}, u32[]{:S(2)}, u32[]{:S(2)}) %all-to-all-start) | async-done | bytes 71712 | tf_op jit(solution)/shard_map/all_to_all | solution.py:267
  20.5 0.9 copy.53
  21.4 3.6 %all-to-all-start.1 = ((bf16[16,6,1536]{2,1,0:T(8,128)(2,1)}), bf16[16,6,1536]{2,1,0:T(8,128)(2,1)S(1)}, u32[]{:S(2)}, u32[]{:S(2)}) async-start(bf16[16,6,1536]{2,1,0:T(8,128)(2,1)} %copy.53), calls=%async_computation.1 | async-start | bytes 786432 | tf_op jit(solution)/shard_map/all_to_all | solution.py:284
  25.0 1.9 %collective-permute-start.1 = (bf16[96,320]{1,0:T(8,128)(2,1)S(1)}, bf16[96,320]{1,0:T(8,128)(2,1)}, u32[]{:S(2)}, u32[]{:S(2)}) collective-permute-start(bf16[96,320]{1,0:T(8,128)(2,1)S(1)} %reshape.195), channel_id=1, source_target_pairs={{0,2},{2,0},{4,6},{6,4},{8,10},{10,8},{12,14},{14,12},{16,18},{18,... | collective-permute-start | bytes 184328 | tf_op jit(solution)/shard_map/ppermute | solution.py:41
  26.9 3.1 %collective-permute-done.1 = bf16[96,320]{1,0:T(8,128)(2,1)} collective-permute-done((bf16[96,320]{1,0:T(8,128)(2,1)S(1)}, bf16[96,320]{1,0:T(8,128)(2,1)}, u32[]{:S(2)}, u32[]{:S(2)}) %collective-permute-start.1) | collective-permute-done | bytes 61472 | tf_op jit(solution)/shard_map/ppermute | solution.py:41
  30.0 0.9 select_bitcast_fusion.1
  30.9 0.7 pad_maximum_fusion.3
  31.6 5.4 %all-to-all-done.1 = bf16[16,6,1536]{2,1,0:T(8,128)(2,1)S(1)} async-done(((bf16[16,6,1536]{2,1,0:T(8,128)(2,1)}), bf16[16,6,1536]{2,1,0:T(8,128)(2,1)S(1)}, u32[]{:S(2)}, u32[]{:S(2)}) %all-to-all-start.1) | async-done | bytes 294944 | tf_op jit(solution)/shard_map/all_to_all | solution.py:284
  37.1 0.8 broadcast_in_dim.34
  37.9 4.2 %all-to-all-start.2 = ((bf16[16,6,1536]{2,1,0:T(8,128)(2,1)}), bf16[16,6,1536]{2,1,0:T(8,128)(2,1)}, u32[]{:S(2)}, u32[]{:S(2)}) async-start(bf16[16,6,1536]{2,1,0:T(8,128)(2,1)} %broadcast_in_dim.34), calls=%async_computation.2 | async-start | bytes 786432 | tf_op jit(solution)/shard_map/all_to_all | solution.py:286
  42.1 1.3 fusion.1
  43.6 1.5 fusion
  45.1 8.1 %all-to-all-done.2 = bf16[16,6,1536]{2,1,0:T(8,128)(2,1)} async-done(((bf16[16,6,1536]{2,1,0:T(8,128)(2,1)}), bf16[16,6,1536]{2,1,0:T(8,128)(2,1)}, u32[]{:S(2)}, u32[]{:S(2)}) %all-to-all-start.2) | async-done | bytes 294944 | tf_op jit(solution)/shard_map/all_to_all | solution.py:286
  53.2 1.1 reshape.194.refs_0_
  54.3 0.6 collective-permute-start.4
  54.9 3.8 %all-to-all-start.3 = ((bf16[8,192,640]{2,1,0:T(8,128)(2,1)}), bf16[8,192,640]{2,1,0:T(8,128)(2,1)S(1)}, u32[]{:S(2)}, u32[]{:S(2)}) async-start(bf16[8,192,640]{2,1,0:T(8,128)(2,1)} %bitcast.47), calls=%async_computation.3 | async-start | bytes 3932160 | tf_op jit(solution)/shard_map/all_to_all | solution.py:293
  58.7 15.3 %collective-permute-done.4 = bf16[320,1536]{1,0:T(8,128)(2,1)} collective-permute-done((bf16[320,1536]{1,0:T(8,128)(2,1)}, bf16[320,1536]{1,0:T(8,128)(2,1)}, u32[]{:S(2)}, u32[]{:S(2)}) %collective-permute-start.4) | collective-permute-done | bytes 983072 | tf_op jit(solution)/shard_map/ppermute | solution.py:305
  74.0 1.6 broadcast_select_fusion.3
  75.6 1.4 pad_maximum_fusion.1.refs_2_
  77.1 1.4 collective-permute-start.6
  78.5 0.8 dynamic_slice.29
  79.7 0.8 copy.55
  80.5 1.7 reshape.200
  82.2 0.9 pad.14.new_ref
  83.2 6.2 %absorb.1.qk_ref = bf16[2304,640]{1,0:T(8,128)(2,1)} custom-call(bf16[96,1536]{1,0:T(8,128)(2,1)S(1)} %reshape.194.refs_0_, bf16[96,1536]{1,0:T(8,128)(2,1)} %collective-permute-done.3.refs_1_, bf16[640,1536]{1,0:T(8,128)(2,1)} %pad_maximum_fusion.1.refs_2_, bf16[640,1536]{1,0:T(8,128)(2,1)} %collective-permute-done.5.refs_3_, ...), custom_call_target="tpu_custom_call" | custom-call | tf_op jit(solution)/shard_map/absorb/pallas_call | solution.py:310
  89.3 13.4 %all-to-all-done.3.slab_ref = bf16[8,192,640]{2,1,0:T(8,128)(2,1)S(1)} async-done(((bf16[8,192,640]{2,1,0:T(8,128)(2,1)}), bf16[8,192,640]{2,1,0:T(8,128)(2,1)S(1)}, u32[]{:S(2)}, u32[]{:S(2)}) %all-to-all-start.3) | async-done | bytes 1966112 | tf_op jit(solution)/shard_map/all_to_all | solution.py:293
  102.7 1.8 %copy-done.1 = bf16[2304,640]{1,0:T(8,128)(2,1)S(1)} copy-done((bf16[2304,640]{1,0:T(8,128)(2,1)S(1)}, bf16[2304,640]{1,0:T(8,128)(2,1)}, u32[]{:S(2)}) %copy-start.1) | copy-done | bytes 2949144
  104.5 8.3 %scores.1 = bf16[8,80,256]{2,1,0:T(8,128)(2,1)} custom-call(bf16[2304,640]{1,0:T(8,128)(2,1)S(1)} %copy-done.1, s32[1,1536]{1,0:T(1,128)S(1)} %reshape.204.slot_ref, s32[1,128]{1,0:T(1,128)S(1)} %pad_bitcast_fusion.new_slot_ref, bf16[8,192,640]{2,1,0:T(8,128)(2,1)S(1)} %all-to-all-done.3.slab_ref, bf16[128,640]{1,0:T(8,128)(2,1)S(1)} %pad.14.new_ref), custom_call_target="tpu_custom_call" | custom-call | tf_op jit(solution)/shard_map/scores/pallas_call | solution.py:329
  112.9 2.9 %broadcast_select_fusion.1 = (bf16[320,1536]{1,0:T(8,128)(2,1)}, bf16[320,1536]{1,0:T(8,128)(2,1)}) fusion(bf16[320,1536]{1,0:T(8,128)(2,1)} %param.16, bf16[320,1536]{1,0:T(8,128)(2,1)} %collective-permute-done.6, pred[]{:T(512)S(6)} %eq.45), kind=kLoop, calls=%fused_computation.18 | loop fusion | flops 983040 | bytes 3932161 | tf_op jit(solution)/shard_map/jit(_where)/select_n | solution.py:301
  115.8 3.5 %all-to-all-start.4 = ((bf16[8,80,256]{2,1,0:T(8,128)(2,1)}), bf16[8,80,256]{2,1,0:T(8,128)(2,1)S(1)}, u32[]{:S(2)}, u32[]{:S(2)}) async-start(bf16[8,80,256]{2,1,0:T(8,128)(2,1)} %scores.1), calls=%async_computation.4 | async-start | bytes 655360 | tf_op jit(solution)/shard_map/all_to_all | solution.py:336
  119.2 2.9 %pad_maximum_fusion.2.refs_0_ = bf16[640,1536]{1,0:T(8,128)(2,1)} fusion(bf16[320,1536]{1,0:T(8,128)(2,1)} %get-tuple-element.30, bf16[320,1536]{1,0:T(8,128)(2,1)} %get-tuple-element.29), kind=kLoop, calls=%fused_computation.10 | loop fusion | flops 3932160 | bytes 3932160 | tf_op jit(solution)/shard_map/concatenate | solution.py:300
  122.4 7.2 %all-to-all-done.4 = bf16[8,80,256]{2,1,0:T(8,128)(2,1)S(1)} async-done(((bf16[8,80,256]{2,1,0:T(8,128)(2,1)}), bf16[8,80,256]{2,1,0:T(8,128)(2,1)S(1)}, u32[]{:S(2)}, u32[]{:S(2)}) %all-to-all-start.4) | async-done | bytes 327712 | tf_op jit(solution)/shard_map/all_to_all | solution.py:336
  129.9 0.7 broadcast_in_dim.63
  130.7 3.7 %all-to-all-start.5 = ((bf16[8,80,256]{2,1,0:T(8,128)(2,1)}), bf16[8,80,256]{2,1,0:T(8,128)(2,1)S(1)}, u32[]{:S(2)}, u32[]{:S(2)}) async-start(bf16[8,80,256]{2,1,0:T(8,128)(2,1)} %broadcast_in_dim.63), calls=%async_computation.5 | async-start | bytes 655360 | tf_op jit(solution)/shard_map/all_to_all | solution.py:352
  134.3 10.2 %all-to-all-done.5.w_ref = bf16[8,80,256]{2,1,0:T(8,128)(2,1)S(1)} async-done(((bf16[8,80,256]{2,1,0:T(8,128)(2,1)}), bf16[8,80,256]{2,1,0:T(8,128)(2,1)S(1)}, u32[]{:S(2)}, u32[]{:S(2)}) %all-to-all-start.5) | async-done | bytes 327712 | tf_op jit(solution)/shard_map/all_to_all | solution.py:352
  144.5 11.5 %values.1 = (bf16[96,1536]{1,0:T(8,128)(2,1)S(1)}, bf16[96,1536]{1,0:T(8,128)(2,1)S(1)}, f32[96,128]{1,0:T(8,128)S(1)}) custom-call(bf16[8,80,256]{2,1,0:T(8,128)(2,1)S(1)} %all-to-all-done.5.w_ref, s32[1,1664]{1,0:T(1,128)S(1)} %pad_add_fusion.slot_ref, f32[1,640]{1,0:T(1,128)S(1)} %reshape.198.refs_4_.gain_ref, ...), custom_call_target="tpu_custom_call" | custom-call | tf_op jit(solution)/shard_map/values/pallas_call | solution.py:358
  156.6 1.1 collective-permute-done.9.theirs_d_ref
  157.8 0.5 join.1
  158.3 17.0 %all_to_all.35 = bf16[16,8,1536]{2,1,0:T(8,128)(2,1)S(1)} all-to-all(bf16[16,8,1536]{2,1,0:T(8,128)(2,1)S(1)} %join.1), channel_id=1, replica_groups=mesh['seq'=16,'tp'=2] {'seq'}, dimensions={0} | all-to-all | bytes 786432 | tf_op jit(solution)/shard_map/all_to_all | solution.py:396
  175.8 0.6 copy.60
  (78 shorter events, 3.8 us)
Async XLA Ops:
  0.0 20.1 %copy-start = (bf16[320,1536]{1,0:T(8,128)(2,1)S(1)}, bf16[320,1536]{1,0:T(8,128)(2,1)}, u32[]{:S(2)}) copy-start(bf16[320,1536]{1,0:T(8,128)(2,1)} %param.17) | copy-start | bytes 2949124
  0.9 2.1 %collective-permute-start = (bf16[6,2560]{1,0:T(8,128)(2,1)S(1)}, bf16[6,2560]{1,0:T(8,128)(2,1)S(1)}, u32[]{:S(2)}, u32[]{:S(2)}) collective-permute-start(bf16[6,2560]{1,0:T(8,128)(2,1)S(1)} %reshape.189), channel_id=1, source_target_pairs={{0,1},{1,0},{2,3},{3,2},{4,5},{5,4},{6,7},{7,6},{8,9},{9,8},{10,11... | collective-permute-start | bytes 92168 | tf_op jit(solution)/shard_map/ppermute | solution.py:235
  4.1 15.6 %all-to-all-start = ((bf16[16,7,320]{2,1,0:T(8,128)(2,1)}), bf16[16,7,320]{2,1,0:T(8,128)(2,1)S(1)}, u32[]{:S(2)}, u32[]{:S(2)}) async-start(bf16[16,7,320]{2,1,0:T(8,128)(2,1)} %pad_maximum_fusion.4), calls=%async_computation | async-start | bytes 196608 | tf_op jit(solution)/shard_map/all_to_all | solution.py:267
  14.3 27.8 %collective-permute-start.2 = (bf16[192,2560]{1,0:T(8,128)(2,1)}, bf16[192,2560]{1,0:T(8,128)(2,1)}, u32[]{:S(2)}, u32[]{:S(2)}) collective-permute-start(bf16[192,2560]{1,0:T(8,128)(2,1)} %dynamic-slice_bitcast_fusion), channel_id=1, source_target_pairs={{0,1},{1,0},{2,3},{3,2},{4,5},{5,4},{6,7},{7,6},{8,9},{9,8},{10,11... | collective-permute-start | bytes 2949128 | tf_op jit(solution)/shard_map/ppermute | solution.py:242
  20.5 21.6 %copy-start.2 = (bf16[384,2560]{1,0:T(8,128)(2,1)S(1)}, bf16[384,2560]{1,0:T(8,128)(2,1)}, u32[]{:S(2)}) copy-start(bf16[384,2560]{1,0:T(8,128)(2,1)} %param.9) | copy-start | bytes 5898244
  21.4 15.6 %all-to-all-start.1 = ((bf16[16,6,1536]{2,1,0:T(8,128)(2,1)}), bf16[16,6,1536]{2,1,0:T(8,128)(2,1)S(1)}, u32[]{:S(2)}, u32[]{:S(2)}) async-start(bf16[16,6,1536]{2,1,0:T(8,128)(2,1)} %copy.53), calls=%async_computation.1 | async-start | bytes 786432 | tf_op jit(solution)/shard_map/all_to_all | solution.py:284
  25.0 5.0 %collective-permute-start.1 = (bf16[96,320]{1,0:T(8,128)(2,1)S(1)}, bf16[96,320]{1,0:T(8,128)(2,1)}, u32[]{:S(2)}, u32[]{:S(2)}) collective-permute-start(bf16[96,320]{1,0:T(8,128)(2,1)S(1)} %reshape.195), channel_id=1, source_target_pairs={{0,2},{2,0},{4,6},{6,4},{8,10},{10,8},{12,14},{14,12},{16,18},{18,... | collective-permute-start | bytes 184328 | tf_op jit(solution)/shard_map/ppermute | solution.py:41
  37.9 15.3 %all-to-all-start.2 = ((bf16[16,6,1536]{2,1,0:T(8,128)(2,1)}), bf16[16,6,1536]{2,1,0:T(8,128)(2,1)}, u32[]{:S(2)}, u32[]{:S(2)}) async-start(bf16[16,6,1536]{2,1,0:T(8,128)(2,1)} %broadcast_in_dim.34), calls=%async_computation.2 | async-start | bytes 786432 | tf_op jit(solution)/shard_map/all_to_all | solution.py:286
  54.3 19.7 %collective-permute-start.4 = (bf16[320,1536]{1,0:T(8,128)(2,1)}, bf16[320,1536]{1,0:T(8,128)(2,1)}, u32[]{:S(2)}, u32[]{:S(2)}) collective-permute-start(bf16[320,1536]{1,0:T(8,128)(2,1)} %param.15), channel_id=1, source_target_pairs={{0,2},{2,0},{4,6},{6,4},{8,10},{10,8},{12,14},{14,12},{16,18},{18,... | collective-permute-start | bytes 2949128 | tf_op jit(solution)/shard_map/ppermute | solution.py:305
  54.9 47.8 %all-to-all-start.3 = ((bf16[8,192,640]{2,1,0:T(8,128)(2,1)}), bf16[8,192,640]{2,1,0:T(8,128)(2,1)S(1)}, u32[]{:S(2)}, u32[]{:S(2)}) async-start(bf16[8,192,640]{2,1,0:T(8,128)(2,1)} %bitcast.47), calls=%async_computation.3 | async-start | bytes 3932160 | tf_op jit(solution)/shard_map/all_to_all | solution.py:293
  75.6 4.1 %copy-start.3 = (bf16[2,96,320]{2,1,0:T(8,128)(2,1)S(1)}, bf16[2,96,320]{2,1,0:T(8,128)(2,1)}, u32[]{:S(2)}) copy-start(bf16[2,96,320]{2,1,0:T(8,128)(2,1)} %pad_maximum_fusion.3) | copy-start | bytes 368644
  77.1 6.1 %collective-permute-start.5 = (bf16[640,1536]{1,0:T(8,128)(2,1)}, bf16[640,1536]{1,0:T(8,128)(2,1)}, u32[]{:S(2)}, u32[]{:S(2)}) collective-permute-start(bf16[640,1536]{1,0:T(8,128)(2,1)} %pad_maximum_fusion.1.refs_2_), channel_id=1, source_target_pairs={{0,1},{1,0},{2,3},{3,2},{4,5},{5,4},{6,7},{7,6},{8,9},{9,8},{10,11... | collective-permute-start | bytes 5898248 | tf_op jit(solution)/shard_map/ppermute | solution.py:235
  77.1 35.8 %collective-permute-start.6 = (bf16[320,1536]{1,0:T(8,128)(2,1)}, bf16[320,1536]{1,0:T(8,128)(2,1)}, u32[]{:S(2)}, u32[]{:S(2)}) collective-permute-start(bf16[320,1536]{1,0:T(8,128)(2,1)} %param.16), channel_id=1, source_target_pairs={{0,2},{2,0},{4,6},{6,4},{8,10},{10,8},{12,14},{14,12},{16,18},{18,... | collective-permute-start | bytes 2949128 | tf_op jit(solution)/shard_map/ppermute | solution.py:305
  79.3 3.8 %collective-permute-start.3 = (bf16[96,1536]{1,0:T(8,128)(2,1)S(1)}, bf16[96,1536]{1,0:T(8,128)(2,1)}, u32[]{:S(2)}, u32[]{:S(2)}) collective-permute-start(bf16[96,1536]{1,0:T(8,128)(2,1)S(1)} %reshape.194.refs_0_), channel_id=1, source_target_pairs={{0,1},{1,0},{2,3},{3,2},{4,5},{5,4},{6,7},{7,6},{8,9},{9,8},{10,11... | collective-permute-start | bytes 884744 | tf_op jit(solution)/shard_map/ppermute | solution.py:235
  102.7 1.8 %copy-start.1 = (bf16[2304,640]{1,0:T(8,128)(2,1)S(1)}, bf16[2304,640]{1,0:T(8,128)(2,1)}, u32[]{:S(2)}) copy-start(bf16[2304,640]{1,0:T(8,128)(2,1)} %absorb.1.qk_ref) | copy-start | bytes 8847364
  115.8 13.9 %all-to-all-start.4 = ((bf16[8,80,256]{2,1,0:T(8,128)(2,1)}), bf16[8,80,256]{2,1,0:T(8,128)(2,1)S(1)}, u32[]{:S(2)}, u32[]{:S(2)}) async-start(bf16[8,80,256]{2,1,0:T(8,128)(2,1)} %scores.1), calls=%async_computation.4 | async-start | bytes 655360 | tf_op jit(solution)/shard_map/all_to_all | solution.py:336
  122.2 22.4 %collective-permute-start.7 = (bf16[640,1536]{1,0:T(8,128)(2,1)}, bf16[640,1536]{1,0:T(8,128)(2,1)}, u32[]{:S(2)}, u32[]{:S(2)}) collective-permute-start(bf16[640,1536]{1,0:T(8,128)(2,1)} %pad_maximum_fusion.2.refs_0_), channel_id=1, source_target_pairs={{0,1},{1,0},{2,3},{3,2},{4,5},{5,4},{6,7},{7,6},{8,9},{9,8},{10,11... | collective-permute-start | bytes 5898248 | tf_op jit(solution)/shard_map/ppermute | solution.py:235
  130.7 13.8 %all-to-all-start.5 = ((bf16[8,80,256]{2,1,0:T(8,128)(2,1)}), bf16[8,80,256]{2,1,0:T(8,128)(2,1)S(1)}, u32[]{:S(2)}, u32[]{:S(2)}) async-start(bf16[8,80,256]{2,1,0:T(8,128)(2,1)} %broadcast_in_dim.63), calls=%async_computation.5 | async-start | bytes 655360 | tf_op jit(solution)/shard_map/all_to_all | solution.py:352
  156.0 1.7 collective-permute-start.8
  156.1 1.6 collective-permute-start.9

commit v3 on v2

--- a/solution.py
+++ b/solution.py
@@ -13,7 +13,7 @@
 SLOTS = 4
 BLOCKS = 4
 NT = (((1,), (1,)), ((), ()))
-VMEM_LIMIT = 48 * 1024 * 1024
+VMEM_LIMIT = 26 * 1024 * 1024
 
 
 def params():
@@ -166,7 +166,7 @@
         put_lanes(mixed_ref, pl.ds(pl.multiple_of(group * depth, depth), depth), mixed * gain)
         return carry
 
-    lax.fori_loop(0, slots // SLOTS, step, 0, unroll=2)
+    lax.fori_loop(0, slots // SLOTS, step, 0, unroll=8)
     rows, per = outs[0].shape[0], outs[0].shape[1] // HEAD
     for piece in range(count):
         for head in range(per):
@@ -283,14 +283,14 @@
     partial = partial.astype(bf16)
     partial = lax.all_to_all(partial, "seq", 0, 0, tiled=True)
     query = jnp.sum(partial.astype(f32), axis=0).astype(bf16)
-    queries = lax.all_to_all(
-        jnp.broadcast_to(query[None], (seq, own_rows, local_width)), "seq", 0, 0, tiled=True
-    ).reshape(rows, local_width)
+    queries = exchange(jnp.broadcast_to(query[None], (shards, own_rows, local_width)))
     state_wide = swap_gather(state_part, "seq", pair, x, x_perm)
     queries, state_wide, message, key_weight, value_weight = lax.optimization_barrier(
         (queries, state_wide, message, key_weight, value_weight)
     )
     slab_in = exchange(message)
+    queries = swap_gather(queries, "seq", pair, x, x_perm)
+    queries = queries.transpose(1, 0, 2, 3).reshape(rows, local_width)
     queries = over_tp(queries)
 
     def join_pair(first, second):
@@ -312,6 +312,11 @@
         out_shape=jax.ShapeDtypeStruct((rows * heads, wide), bf16),
         scratch_shapes=[pltpu.VMEM((-(-wide // 128), rows * heads, 128), f32)],
         compiler_params=params(),
+        cost_estimate=pl.CostEstimate(
+            flops=2 * rows * heads * HEAD * wide,
+            bytes_accessed=2 * (wide + rows) * heads * HEAD,
+            transcendentals=0,
+        ),
         name="absorb",
     )(*queries, *keys_full, gain)
 

time: 178 us -> 170 us (0.955)
  waiting for transfers between devices: 68.2 us -> 63.5 us
  Pallas kernels: 26.6 us -> 23.7 us
    all_to_all x1, waiting for transfers between devices: 13.4 us -> 5.01 us  [on_device(): slab_in = exchange(message)]
    ppermute x1 -> x2, waiting for transfers between devices: 3.1 us -> 7.85 us  [swap_gather(): other = lax.ppermute(values, axis, perm)]
    all_to_all x1, waiting for transfers between devices: 8.07 us -> 4.76 us  [on_device(): exchange(jnp.broadcast_to(query[None], (shards, own_rows, local_width)))]
    ppermute x2, waiting for transfers between devices: 15.3 us -> 17.1 us  [from_pair(): return values if pair == 1 else lax.ppermute(values, 'seq', x_perm)]
    unnamed x10 -> x12, local copies, waits for them, and re-layouts: 2.71 us -> 4.31 us
  transfers between devices with their start and end apart: 16 -> 17, of which waited for: 9 -> 11; matrix products, arithmetic and copies ran while one was open for 13% -> 14% of each run, Pallas kernels for 8% -> 8%
where the time goes in v3:
time: 170 us; the launch traced here: 169 us
  waiting for transfers between devices  63.5 us (37%)
  starting transfers between devices  31.8 us (19%)
  Pallas kernels  23.7 us (14%)
  other arithmetic  17.3 us (10%)
  blocking collectives  17.3 us (10%)
  local copies, waits for them, and re-layouts  14.3 us (8%)
    all_to_all x1, blocking collectives, on_device(): got = lax.all_to_all(sent, axes, 0, 0, tiled=True)  17.3 us
    ppermute x2, waiting for transfers between devices, from_pair(): return values if pair == 1 else lax.ppermute(values, 'seq', x_perm)  17.1 us
    pallas_call x1, Pallas kernels, on_device(): pl.pallas_call(functools.partial(value_kernel, slots, per_slot, new_cols,...  10.3 us
    all_to_all x1, waiting for transfers between devices, on_device(): lax.all_to_all(jnp.broadcast_to(ready[None], (shards, out_rows, width)),...  10.2 us
    pallas_call x1, Pallas kernels, on_device(): pl.pallas_call(functools.partial(score_kernel, slots, per_slot, new_cols)...  8.34 us
    all_to_all x1, starting transfers between devices, on_device(): got = lax.all_to_all(sent, 'seq', 0, 0, tiled=True)  7.88 us
    ppermute x2, waiting for transfers between devices, swap_gather(): other = lax.ppermute(values, axis, perm)  7.85 us
    all_to_all x1, waiting for transfers between devices, on_device(): lax.all_to_all(partial, 'seq', 0, 0, tiled=True, axis_index_groups=groups)  7.26 us
  transfers between devices with their start and end apart: 17, of which 11 were waited for; matrix products, arithmetic and copies ran while one was open for 14% of the time, Pallas kernels for 8%

profile of v3, /device:TPU:0, one launch (start us, length us, event | category | flops | bytes accessed | tf_op | source)
XLA Modules:
  0.0 168.8 jit_solution(8509358092015993788)
XLA Ops:
  0.0 0.9 copy.51
  1.4 0.7 reduce.5
  2.2 0.7 select_reduce_fusion
  3.5 0.7 pad_maximum_fusion.4
  4.1 7.9 %all-to-all-start = ((bf16[16,7,320]{2,1,0:T(8,128)(2,1)}), bf16[16,7,320]{2,1,0:T(8,128)(2,1)S(1)}, u32[]{:S(2)}, u32[]{:S(2)}) async-start(bf16[16,7,320]{2,1,0:T(8,128)(2,1)} %pad_maximum_fusion.4), calls=%async_computation | async-start | bytes 196608 | tf_op jit(solution)/shard_map/all_to_all | solution.py:267
  12.0 2.2 %dynamic-slice_bitcast_fusion = bf16[192,2560]{1,0:T(8,128)(2,1)} fusion(bf16[2,192,2560]{2,1,0:T(8,128)(2,1)} %bitcast.56, s32[]{:T(128)S(6)} %select_n.166), kind=kLoop, calls=%fused_computation.16 | loop fusion | bytes 1966084 | tf_op jit(solution)/shard_map/jit(dynamic_index_in_dim)/squeeze | solution.py:243
  14.5 0.8 dynamic_slice.26
  15.2 4.5 %all-to-all-done = bf16[16,7,320]{2,1,0:T(8,128)(2,1)S(1)} async-done(((bf16[16,7,320]{2,1,0:T(8,128)(2,1)}), bf16[16,7,320]{2,1,0:T(8,128)(2,1)S(1)}, u32[]{:S(2)}, u32[]{:S(2)}) %all-to-all-start) | async-done | bytes 71712 | tf_op jit(solution)/shard_map/all_to_all | solution.py:267
  20.5 0.9 copy.57
  21.4 3.6 %all-to-all-start.1 = ((bf16[16,6,1536]{2,1,0:T(8,128)(2,1)}), bf16[16,6,1536]{2,1,0:T(8,128)(2,1)S(1)}, u32[]{:S(2)}, u32[]{:S(2)}) async-start(bf16[16,6,1536]{2,1,0:T(8,128)(2,1)} %copy.57), calls=%async_computation.1 | async-start | bytes 786432 | tf_op jit(solution)/shard_map/all_to_all | solution.py:284
  25.0 1.9 %collective-permute-start.1 = (bf16[96,320]{1,0:T(8,128)(2,1)S(1)}, bf16[96,320]{1,0:T(8,128)(2,1)}, u32[]{:S(2)}, u32[]{:S(2)}) collective-permute-start(bf16[96,320]{1,0:T(8,128)(2,1)S(1)} %reshape.194), channel_id=1, source_target_pairs={{0,2},{2,0},{4,6},{6,4},{8,10},{10,8},{12,14},{14,12},{16,18},{18,... | collective-permute-start | bytes 184328 | tf_op jit(solution)/shard_map/ppermute | solution.py:41
  26.9 3.1 %collective-permute-done.1 = bf16[96,320]{1,0:T(8,128)(2,1)} collective-permute-done((bf16[96,320]{1,0:T(8,128)(2,1)S(1)}, bf16[96,320]{1,0:T(8,128)(2,1)}, u32[]{:S(2)}, u32[]{:S(2)}) %collective-permute-start.1) | collective-permute-done | bytes 61472 | tf_op jit(solution)/shard_map/ppermute | solution.py:41
  30.0 0.9 select_bitcast_fusion.3
  30.9 0.7 pad_maximum_fusion.3
  31.6 5.4 %all-to-all-done.1 = bf16[16,6,1536]{2,1,0:T(8,128)(2,1)S(1)} async-done(((bf16[16,6,1536]{2,1,0:T(8,128)(2,1)}), bf16[16,6,1536]{2,1,0:T(8,128)(2,1)S(1)}, u32[]{:S(2)}, u32[]{:S(2)}) %all-to-all-start.1) | async-done | bytes 294944 | tf_op jit(solution)/shard_map/all_to_all | solution.py:284
  37.1 0.7 broadcast_in_dim.34
  37.8 3.5 %all-to-all-start.2 = ((bf16[8,6,1536]{2,1,0:T(8,128)(2,1)}), bf16[8,6,1536]{2,1,0:T(8,128)(2,1)S(1)}, u32[]{:S(2)}, u32[]{:S(2)}) async-start(bf16[8,6,1536]{2,1,0:T(8,128)(2,1)} %broadcast_in_dim.34), calls=%async_computation.2 | async-start | bytes 393216 | tf_op jit(solution)/shard_map/all_to_all | solution.py:286
  41.3 1.3 fusion.1
  42.8 1.5 fusion
  44.3 4.8 %all-to-all-done.2 = bf16[8,6,1536]{2,1,0:T(8,128)(2,1)S(1)} async-done(((bf16[8,6,1536]{2,1,0:T(8,128)(2,1)}), bf16[8,6,1536]{2,1,0:T(8,128)(2,1)S(1)}, u32[]{:S(2)}, u32[]{:S(2)}) %all-to-all-start.2) | async-done | bytes 147488 | tf_op jit(solution)/shard_map/all_to_all | solution.py:286
  49.0 0.6 collective-permute-start.5
  49.6 3.8 %all-to-all-start.3 = ((bf16[8,192,640]{2,1,0:T(8,128)(2,1)}), bf16[8,192,640]{2,1,0:T(8,128)(2,1)S(1)}, u32[]{:S(2)}, u32[]{:S(2)}) async-start(bf16[8,192,640]{2,1,0:T(8,128)(2,1)} %bitcast.55), calls=%async_computation.3 | async-start | bytes 3932160 | tf_op jit(solution)/shard_map/all_to_all | solution.py:291
  53.4 17.1 %collective-permute-done.5 = bf16[320,1536]{1,0:T(8,128)(2,1)} collective-permute-done((bf16[320,1536]{1,0:T(8,128)(2,1)}, bf16[320,1536]{1,0:T(8,128)(2,1)}, u32[]{:S(2)}, u32[]{:S(2)}) %collective-permute-start.5) | collective-permute-done | bytes 983072 | tf_op jit(solution)/shard_map/ppermute | solution.py:305
  70.5 1.6 broadcast_select_fusion.3
  72.1 1.4 pad_maximum_fusion.1.refs_2_
  73.5 0.6 collective-permute-start.3
  74.1 0.8 dynamic_slice.29
  74.9 1.5 collective-permute-start.7
  76.5 4.8 %collective-permute-done.3 = bf16[8,6,1536]{2,1,0:T(8,128)(2,1)S(1)} collective-permute-done((bf16[8,6,1536]{2,1,0:T(8,128)(2,1)S(1)}, bf16[8,6,1536]{2,1,0:T(8,128)(2,1)S(1)}, u32[]{:S(2)}, u32[]{:S(2)}) %collective-permute-start.3) | collective-permute-done | bytes 147488 | tf_op jit(solution)/shard_map/ppermute | solution.py:41
  81.2 0.8 maximum_bitcast_fusion
  82.1 1.1 reshape.197.refs_0_
  83.4 1.0 copy.60
  85.0 4.6 %absorb.1.qk_ref = bf16[2304,640]{1,0:T(8,128)(2,1)S(1)} custom-call(bf16[96,1536]{1,0:T(8,128)(2,1)S(1)} %reshape.197.refs_0_, bf16[96,1536]{1,0:T(8,128)(2,1)} %collective-permute-done.4.refs_1_, bf16[640,1536]{1,0:T(8,128)(2,1)} %pad_maximum_fusion.1.refs_2_, bf16[640,1536]{1,0:T(8,128)(2,1)} %collective-permute-done.6.refs_3_, ...), custom_call_target="tpu_custom_call" | custom-call | flops 377487360 | bytes 4521984 | tf_op jit(solution)/shard_map/absorb/pallas_call | solution.py:310
  89.5 1.6 copy-done.1
  91.2 5.0 %all-to-all-done.3.slab_ref = bf16[8,192,640]{2,1,0:T(8,128)(2,1)S(1)} async-done(((bf16[8,192,640]{2,1,0:T(8,128)(2,1)}), bf16[8,192,640]{2,1,0:T(8,128)(2,1)S(1)}, u32[]{:S(2)}, u32[]{:S(2)}) %all-to-all-start.3) | async-done | bytes 1966112 | tf_op jit(solution)/shard_map/all_to_all | solution.py:291
  96.2 1.8 %copy-done.2 = bf16[2304,640]{1,0:T(8,128)(2,1)S(1)} copy-done((bf16[2304,640]{1,0:T(8,128)(2,1)S(1)}, bf16[2304,640]{1,0:T(8,128)(2,1)}, u32[]{:S(2)}) %copy-start.2) | copy-done | bytes 2949144
  98.0 8.3 %scores.1 = bf16[8,80,256]{2,1,0:T(8,128)(2,1)} custom-call(bf16[2304,640]{1,0:T(8,128)(2,1)S(1)} %copy-done.2, s32[1,1536]{1,0:T(1,128)S(1)} %reshape.204.slot_ref, s32[1,128]{1,0:T(1,128)S(1)} %pad_bitcast_fusion.new_slot_ref, bf16[8,192,640]{2,1,0:T(8,128)(2,1)S(1)} %all-to-all-done.3.slab_ref, bf16[128,640]{1,0:T(8,128)(2,1)S(1)} %pad.14.new_ref), custom_call_target="tpu_custom_call" | custom-call | tf_op jit(solution)/shard_map/scores/pallas_call | solution.py:334
  106.3 2.6 %broadcast_select_fusion.1 = (bf16[320,1536]{1,0:T(8,128)(2,1)}, bf16[320,1536]{1,0:T(8,128)(2,1)}) fusion(bf16[320,1536]{1,0:T(8,128)(2,1)S(1)} %copy-done.4, bf16[320,1536]{1,0:T(8,128)(2,1)} %collective-permute-done.7, pred[]{:T(512)S(6)} %eq.45), kind=kLoop, calls=%fused_computation.18 | loop fusion | flops 983040 | bytes 3932161 | tf_op jit(solution)/shard_map/jit(_where)/select_n | solution.py:301
  109.0 3.6 %all-to-all-start.4 = ((bf16[8,80,256]{2,1,0:T(8,128)(2,1)}), bf16[8,80,256]{2,1,0:T(8,128)(2,1)S(1)}, u32[]{:S(2)}, u32[]{:S(2)}) async-start(bf16[8,80,256]{2,1,0:T(8,128)(2,1)} %scores.1), calls=%async_computation.4 | async-start | bytes 655360 | tf_op jit(solution)/shard_map/all_to_all | solution.py:341
  112.6 2.9 %pad_maximum_fusion.2.refs_0_ = bf16[640,1536]{1,0:T(8,128)(2,1)} fusion(bf16[320,1536]{1,0:T(8,128)(2,1)} %get-tuple-element.30, bf16[320,1536]{1,0:T(8,128)(2,1)} %get-tuple-element.29), kind=kLoop, calls=%fused_computation.10 | loop fusion | flops 3932160 | bytes 3932160 | tf_op jit(solution)/shard_map/concatenate | solution.py:300
  115.8 7.3 %all-to-all-done.4 = bf16[8,80,256]{2,1,0:T(8,128)(2,1)S(1)} async-done(((bf16[8,80,256]{2,1,0:T(8,128)(2,1)}), bf16[8,80,256]{2,1,0:T(8,128)(2,1)S(1)}, u32[]{:S(2)}, u32[]{:S(2)}) %all-to-all-start.4) | async-done | bytes 327712 | tf_op jit(solution)/shard_map/all_to_all | solution.py:341
  123.3 0.7 broadcast_in_dim.63
  124.0 3.7 %all-to-all-start.5 = ((bf16[8,80,256]{2,1,0:T(8,128)(2,1)}), bf16[8,80,256]{2,1,0:T(8,128)(2,1)S(1)}, u32[]{:S(2)}, u32[]{:S(2)}) async-start(bf16[8,80,256]{2,1,0:T(8,128)(2,1)} %broadcast_in_dim.63), calls=%async_computation.5 | async-start | bytes 655360 | tf_op jit(solution)/shard_map/all_to_all | solution.py:357
  127.7 10.2 %all-to-all-done.5.w_ref = bf16[8,80,256]{2,1,0:T(8,128)(2,1)S(1)} async-done(((bf16[8,80,256]{2,1,0:T(8,128)(2,1)}), bf16[8,80,256]{2,1,0:T(8,128)(2,1)S(1)}, u32[]{:S(2)}, u32[]{:S(2)}) %all-to-all-start.5) | async-done | bytes 327712 | tf_op jit(solution)/shard_map/all_to_all | solution.py:357
  137.9 10.3 %values.1 = (bf16[96,1536]{1,0:T(8,128)(2,1)S(1)}, bf16[96,1536]{1,0:T(8,128)(2,1)S(1)}, f32[96,128]{1,0:T(8,128)S(1)}) custom-call(bf16[8,80,256]{2,1,0:T(8,128)(2,1)S(1)} %all-to-all-done.5.w_ref, s32[1,1664]{1,0:T(1,128)S(1)} %pad_add_fusion.slot_ref, f32[1,640]{1,0:T(1,128)S(1)} %reshape.198.refs_4_.gain_ref, ...), custom_call_target="tpu_custom_call" | custom-call | tf_op jit(solution)/shard_map/values/pallas_call | solution.py:363
  148.7 1.1 collective-permute-done.10.theirs_d_ref
  150.4 17.3 %all_to_all.35 = bf16[16,8,1536]{2,1,0:T(8,128)(2,1)S(1)} all-to-all(bf16[16,8,1536]{2,1,0:T(8,128)(2,1)S(1)} %join.1), channel_id=1, replica_groups=mesh['seq'=16,'tp'=2] {'seq'}, dimensions={0} | all-to-all | bytes 786432 | tf_op jit(solution)/shard_map/all_to_all | solution.py:401
  168.2 0.6 copy.65
  (84 shorter events, 5.2 us)
Async XLA Ops:
  0.0 20.1 %copy-start = (bf16[320,1536]{1,0:T(8,128)(2,1)S(1)}, bf16[320,1536]{1,0:T(8,128)(2,1)}, u32[]{:S(2)}) copy-start(bf16[320,1536]{1,0:T(8,128)(2,1)} %param.17) | copy-start | bytes 2949124
  0.9 2.1 %collective-permute-start = (bf16[6,2560]{1,0:T(8,128)(2,1)S(1)}, bf16[6,2560]{1,0:T(8,128)(2,1)S(1)}, u32[]{:S(2)}, u32[]{:S(2)}) collective-permute-start(bf16[6,2560]{1,0:T(8,128)(2,1)S(1)} %reshape.189), channel_id=1, source_target_pairs={{0,1},{1,0},{2,3},{3,2},{4,5},{5,4},{6,7},{7,6},{8,9},{9,8},{10,11... | collective-permute-start | bytes 92168 | tf_op jit(solution)/shard_map/ppermute | solution.py:235
  4.1 15.6 %all-to-all-start = ((bf16[16,7,320]{2,1,0:T(8,128)(2,1)}), bf16[16,7,320]{2,1,0:T(8,128)(2,1)S(1)}, u32[]{:S(2)}, u32[]{:S(2)}) async-start(bf16[16,7,320]{2,1,0:T(8,128)(2,1)} %pad_maximum_fusion.4), calls=%async_computation | async-start | bytes 196608 | tf_op jit(solution)/shard_map/all_to_all | solution.py:267
  14.3 27.0 %collective-permute-start.2 = (bf16[192,2560]{1,0:T(8,128)(2,1)}, bf16[192,2560]{1,0:T(8,128)(2,1)}, u32[]{:S(2)}, u32[]{:S(2)}) collective-permute-start(bf16[192,2560]{1,0:T(8,128)(2,1)} %dynamic-slice_bitcast_fusion), channel_id=1, source_target_pairs={{0,1},{1,0},{2,3},{3,2},{4,5},{5,4},{6,7},{7,6},{8,9},{9,8},{10,11... | collective-permute-start | bytes 2949128 | tf_op jit(solution)/shard_map/ppermute | solution.py:242
  20.5 20.8 %copy-start.3 = (bf16[384,2560]{1,0:T(8,128)(2,1)S(1)}, bf16[384,2560]{1,0:T(8,128)(2,1)}, u32[]{:S(2)}) copy-start(bf16[384,2560]{1,0:T(8,128)(2,1)} %param.9) | copy-start | bytes 5898244
  21.4 15.6 %all-to-all-start.1 = ((bf16[16,6,1536]{2,1,0:T(8,128)(2,1)}), bf16[16,6,1536]{2,1,0:T(8,128)(2,1)S(1)}, u32[]{:S(2)}, u32[]{:S(2)}) async-start(bf16[16,6,1536]{2,1,0:T(8,128)(2,1)} %copy.57), calls=%async_computation.1 | async-start | bytes 786432 | tf_op jit(solution)/shard_map/all_to_all | solution.py:284
  25.0 5.0 %collective-permute-start.1 = (bf16[96,320]{1,0:T(8,128)(2,1)S(1)}, bf16[96,320]{1,0:T(8,128)(2,1)}, u32[]{:S(2)}, u32[]{:S(2)}) collective-permute-start(bf16[96,320]{1,0:T(8,128)(2,1)S(1)} %reshape.194), channel_id=1, source_target_pairs={{0,2},{2,0},{4,6},{6,4},{8,10},{10,8},{12,14},{14,12},{16,18},{18,... | collective-permute-start | bytes 184328 | tf_op jit(solution)/shard_map/ppermute | solution.py:41
  37.8 11.3 %all-to-all-start.2 = ((bf16[8,6,1536]{2,1,0:T(8,128)(2,1)}), bf16[8,6,1536]{2,1,0:T(8,128)(2,1)S(1)}, u32[]{:S(2)}, u32[]{:S(2)}) async-start(bf16[8,6,1536]{2,1,0:T(8,128)(2,1)} %broadcast_in_dim.34), calls=%async_computation.2 | async-start | bytes 393216 | tf_op jit(solution)/shard_map/all_to_all | solution.py:286
  49.0 21.4 %collective-permute-start.5 = (bf16[320,1536]{1,0:T(8,128)(2,1)}, bf16[320,1536]{1,0:T(8,128)(2,1)}, u32[]{:S(2)}, u32[]{:S(2)}) collective-permute-start(bf16[320,1536]{1,0:T(8,128)(2,1)} %param.15), channel_id=1, source_target_pairs={{0,2},{2,0},{4,6},{6,4},{8,10},{10,8},{12,14},{14,12},{16,18},{18,... | collective-permute-start | bytes 2949128 | tf_op jit(solution)/shard_map/ppermute | solution.py:305
  49.6 46.6 %all-to-all-start.3 = ((bf16[8,192,640]{2,1,0:T(8,128)(2,1)}), bf16[8,192,640]{2,1,0:T(8,128)(2,1)S(1)}, u32[]{:S(2)}, u32[]{:S(2)}) async-start(bf16[8,192,640]{2,1,0:T(8,128)(2,1)} %bitcast.55), calls=%async_computation.3 | async-start | bytes 3932160 | tf_op jit(solution)/shard_map/all_to_all | solution.py:291
  73.5 11.5 %collective-permute-start.6 = (bf16[640,1536]{1,0:T(8,128)(2,1)}, bf16[640,1536]{1,0:T(8,128)(2,1)}, u32[]{:S(2)}, u32[]{:S(2)}) collective-permute-start(bf16[640,1536]{1,0:T(8,128)(2,1)} %pad_maximum_fusion.1.refs_2_), channel_id=1, source_target_pairs={{0,1},{1,0},{2,3},{3,2},{4,5},{5,4},{6,7},{7,6},{8,9},{9,8},{10,11... | collective-permute-start | bytes 5898248 | tf_op jit(solution)/shard_map/ppermute | solution.py:235
  73.5 7.7 %collective-permute-start.3 = (bf16[8,6,1536]{2,1,0:T(8,128)(2,1)S(1)}, bf16[8,6,1536]{2,1,0:T(8,128)(2,1)S(1)}, u32[]{:S(2)}, u32[]{:S(2)}) collective-permute-start(bf16[8,6,1536]{2,1,0:T(8,128)(2,1)S(1)} %all-to-all-done.2), channel_id=1, source_target_pairs={{0,2},{2,0},{4,6},{6,4},{8,10},{10,8},{12,14},{14,12},{16,18},{18,... | collective-permute-start | bytes 442376 | tf_op jit(solution)/shard_map/ppermute | solution.py:41
  74.9 31.4 %collective-permute-start.7 = (bf16[320,1536]{1,0:T(8,128)(2,1)}, bf16[320,1536]{1,0:T(8,128)(2,1)}, u32[]{:S(2)}, u32[]{:S(2)}) collective-permute-start(bf16[320,1536]{1,0:T(8,128)(2,1)} %param.16), channel_id=1, source_target_pairs={{0,2},{2,0},{4,6},{6,4},{8,10},{10,8},{12,14},{14,12},{16,18},{18,... | collective-permute-start | bytes 2949128 | tf_op jit(solution)/shard_map/ppermute | solution.py:305
  83.2 1.8 %collective-permute-start.4 = (bf16[96,1536]{1,0:T(8,128)(2,1)S(1)}, bf16[96,1536]{1,0:T(8,128)(2,1)}, u32[]{:S(2)}, u32[]{:S(2)}) collective-permute-start(bf16[96,1536]{1,0:T(8,128)(2,1)S(1)} %reshape.197.refs_0_), channel_id=1, source_target_pairs={{0,1},{1,0},{2,3},{3,2},{4,5},{5,4},{6,7},{7,6},{8,9},{9,8},{10,11... | collective-permute-start | bytes 884744 | tf_op jit(solution)/shard_map/ppermute | solution.py:235
  89.5 1.6 copy-start.1
  96.2 1.8 %copy-start.2 = (bf16[2304,640]{1,0:T(8,128)(2,1)S(1)}, bf16[2304,640]{1,0:T(8,128)(2,1)}, u32[]{:S(2)}) copy-start(bf16[2304,640]{1,0:T(8,128)(2,1)} %copy-done.1) | copy-start | bytes 8847364
  98.0 8.3 %copy-start.4 = (bf16[320,1536]{1,0:T(8,128)(2,1)S(1)}, bf16[320,1536]{1,0:T(8,128)(2,1)}, u32[]{:S(2)}) copy-start(bf16[320,1536]{1,0:T(8,128)(2,1)} %param.16) | copy-start | bytes 2949124
  109.0 14.1 %all-to-all-start.4 = ((bf16[8,80,256]{2,1,0:T(8,128)(2,1)}), bf16[8,80,256]{2,1,0:T(8,128)(2,1)S(1)}, u32[]{:S(2)}, u32[]{:S(2)}) async-start(bf16[8,80,256]{2,1,0:T(8,128)(2,1)} %scores.1), calls=%async_computation.4 | async-start | bytes 655360 | tf_op jit(solution)/shard_map/all_to_all | solution.py:341
  115.5 22.4 %collective-permute-start.8 = (bf16[640,1536]{1,0:T(8,128)(2,1)}, bf16[640,1536]{1,0:T(8,128)(2,1)}, u32[]{:S(2)}, u32[]{:S(2)}) collective-permute-start(bf16[640,1536]{1,0:T(8,128)(2,1)} %pad_maximum_fusion.2.refs_0_), channel_id=1, source_target_pairs={{0,1},{1,0},{2,3},{3,2},{4,5},{5,4},{6,7},{7,6},{8,9},{9,8},{10,11... | collective-permute-start | bytes 5898248 | tf_op jit(solution)/shard_map/ppermute | solution.py:235
  124.0 13.8 %all-to-all-start.5 = ((bf16[8,80,256]{2,1,0:T(8,128)(2,1)}), bf16[8,80,256]{2,1,0:T(8,128)(2,1)S(1)}, u32[]{:S(2)}, u32[]{:S(2)}) async-start(bf16[8,80,256]{2,1,0:T(8,128)(2,1)} %broadcast_in_dim.63), calls=%async_computation.5 | async-start | bytes 655360 | tf_op jit(solution)/shard_map/all_to_all | solution.py:357
  148.1 1.7 %collective-permute-start.9 = (bf16[96,1536]{1,0:T(8,128)(2,1)S(1)}, bf16[96,1536]{1,0:T(8,128)(2,1)S(1)}, u32[]{:S(2)}, u32[]{:S(2)}) collective-permute-start(bf16[96,1536]{1,0:T(8,128)(2,1)S(1)} %get-tuple-element.23), channel_id=1, source_target_pairs={{0,1},{1,0},{2,3},{3,2},{4,5},{5,4},{6,7},{7,6},{8,9},{9,8},{10,11... | collective-permute-start | bytes 884744 | tf_op jit(solution)/shard_map/ppermute | solution.py:388
  148.2 1.6 collective-permute-start.10

commit v4 on v3

--- a/solution.py
+++ b/solution.py
@@ -339,7 +339,9 @@
     )(absorbed, slot_row, new_row, slab_in, state_wide)
     partial, value_other = lax.optimization_barrier((partial, value_other))
     partial = lax.all_to_all(partial, "seq", 0, 0, tiled=True, axis_index_groups=groups)
-    values_full = over_tp(join_pair(value_weight, value_other))
+    values_full = [
+        join_pair(*blocks) for blocks in zip(over_tp(value_weight), over_tp(value_other))
+    ]
     summed = jnp.sum(partial.astype(f32), axis=0)
     mean = (summed[per_slot] + summed[per_slot + 1]) / model
     factor = lax.rsqrt(mean + 1e-06)[None]

time: 170 us -> 168 us (0.988)
  waiting for transfers between devices: 63.5 us -> 55.9 us
  local copies, waits for them, and re-layouts: 14.3 us -> 19 us
  other arithmetic: 17.3 us -> 20.2 us
  Pallas kernels: 23.7 us -> 21.6 us
    all_to_all x1, waiting for transfers between devices: 10.2 us -> 5.98 us  [on_device(): lax.all_to_all(jnp.broadcast_to(ready[None], (shards, out_rows, width)),...]
    unnamed x12 -> x30, local copies, waits for them, and re-layouts: 4.31 us -> 7.71 us
    all_to_all x1, waiting for transfers between devices: 5.01 us -> 2.84 us  [on_device(): slab_in = exchange(message)]
    pallas_call x1, Pallas kernels: 10.3 us -> 8.12 us  [on_device(): pl.pallas_call(functools.partial(value_kernel, slots, per_slot, new_cols,...]
    select_n x2 -> x3, other arithmetic: 4.26 us -> 6.29 us  [join_pair(): jnp.where(low, first, second)]
  transfers between devices with their start and end apart: 17 -> 18, of which waited for: 11 -> 10; matrix products, arithmetic and copies ran while one was open for 14% -> 18% of each run, Pallas kernels for 8% -> 8%
where the time goes in v4:
time: 168 us; the launch traced here: 167 us
  waiting for transfers between devices  55.9 us (33%)
  starting transfers between devices  32.4 us (19%)
  Pallas kernels  21.6 us (13%)
  other arithmetic  20.2 us (12%)
  local copies, waits for them, and re-layouts  19 us (11%)
  blocking collectives  17.3 us (10%)
    all_to_all x1, blocking collectives, on_device(): got = lax.all_to_all(sent, axes, 0, 0, tiled=True)  17.3 us
    ppermute x2, waiting for transfers between devices, from_pair(): return values if pair == 1 else lax.ppermute(values, 'seq', x_perm)  17.1 us
    pallas_call x1, Pallas kernels, on_device(): pl.pallas_call(functools.partial(score_kernel, slots, per_slot, new_cols)...  8.37 us
    pallas_call x1, Pallas kernels, on_device(): pl.pallas_call(functools.partial(value_kernel, slots, per_slot, new_cols,...  8.12 us
    all_to_all x1, starting transfers between devices, on_device(): got = lax.all_to_all(sent, 'seq', 0, 0, tiled=True)  7.88 us
    unnamed x30, local copies, waits for them, and re-layouts  7.71 us
    all_to_all x1, waiting for transfers between devices, on_device(): lax.all_to_all(partial, 'seq', 0, 0, tiled=True, axis_index_groups=groups)  7.43 us
    ppermute x2, waiting for transfers between devices, swap_gather(): other = lax.ppermute(values, axis, perm)  6.75 us
  transfers between devices with their start and end apart: 18, of which 10 were waited for; matrix products, arithmetic and copies ran while one was open for 18% of the time, Pallas kernels for 8%

profile of v4, /device:TPU:0, one launch (start us, length us, event | category | flops | bytes accessed | tf_op | source)
XLA Modules:
  0.0 167.3 jit_solution(11813684769262893750)
XLA Ops:
  0.0 0.9 copy.51
  1.4 0.7 reduce.5
  2.2 0.7 select_reduce_fusion
  3.5 0.7 pad_maximum_fusion.5
  4.1 7.9 %all-to-all-start = ((bf16[16,7,320]{2,1,0:T(8,128)(2,1)}), bf16[16,7,320]{2,1,0:T(8,128)(2,1)S(1)}, u32[]{:S(2)}, u32[]{:S(2)}) async-start(bf16[16,7,320]{2,1,0:T(8,128)(2,1)} %pad_maximum_fusion.5), calls=%async_computation | async-start | bytes 196608 | tf_op jit(solution)/shard_map/all_to_all | solution.py:267
  12.0 2.2 %dynamic-slice_bitcast_fusion = bf16[192,2560]{1,0:T(8,128)(2,1)} fusion(bf16[2,192,2560]{2,1,0:T(8,128)(2,1)} %bitcast.56, s32[]{:T(128)S(6)} %select_n.174), kind=kLoop, calls=%fused_computation.17 | loop fusion | bytes 1966084 | tf_op jit(solution)/shard_map/jit(dynamic_index_in_dim)/squeeze | solution.py:243
  14.5 0.8 dynamic_slice.26
  15.3 4.5 %all-to-all-done = bf16[16,7,320]{2,1,0:T(8,128)(2,1)S(1)} async-done(((bf16[16,7,320]{2,1,0:T(8,128)(2,1)}), bf16[16,7,320]{2,1,0:T(8,128)(2,1)S(1)}, u32[]{:S(2)}, u32[]{:S(2)}) %all-to-all-start) | async-done | bytes 71712 | tf_op jit(solution)/shard_map/all_to_all | solution.py:267
  20.5 0.9 copy.57
  21.4 3.6 %all-to-all-start.1 = ((bf16[16,6,1536]{2,1,0:T(8,128)(2,1)}), bf16[16,6,1536]{2,1,0:T(8,128)(2,1)S(1)}, u32[]{:S(2)}, u32[]{:S(2)}) async-start(bf16[16,6,1536]{2,1,0:T(8,128)(2,1)} %copy.57), calls=%async_computation.1 | async-start | bytes 786432 | tf_op jit(solution)/shard_map/all_to_all | solution.py:284
  25.0 1.9 %collective-permute-start.1 = (bf16[96,320]{1,0:T(8,128)(2,1)S(1)}, bf16[96,320]{1,0:T(8,128)(2,1)}, u32[]{:S(2)}, u32[]{:S(2)}) collective-permute-start(bf16[96,320]{1,0:T(8,128)(2,1)S(1)} %reshape.194), channel_id=1, source_target_pairs={{0,2},{2,0},{4,6},{6,4},{8,10},{10,8},{12,14},{14,12},{16,18},{18,... | collective-permute-start | bytes 184328 | tf_op jit(solution)/shard_map/ppermute | solution.py:41
  26.9 3.1 %collective-permute-done.1 = bf16[96,320]{1,0:T(8,128)(2,1)} collective-permute-done((bf16[96,320]{1,0:T(8,128)(2,1)S(1)}, bf16[96,320]{1,0:T(8,128)(2,1)}, u32[]{:S(2)}, u32[]{:S(2)}) %collective-permute-start.1) | collective-permute-done | bytes 61472 | tf_op jit(solution)/shard_map/ppermute | solution.py:41
  30.0 0.9 select_bitcast_fusion.3
  30.9 0.7 pad_maximum_fusion.4
  31.6 5.4 %all-to-all-done.1 = bf16[16,6,1536]{2,1,0:T(8,128)(2,1)S(1)} async-done(((bf16[16,6,1536]{2,1,0:T(8,128)(2,1)}), bf16[16,6,1536]{2,1,0:T(8,128)(2,1)S(1)}, u32[]{:S(2)}, u32[]{:S(2)}) %all-to-all-start.1) | async-done | bytes 294944 | tf_op jit(solution)/shard_map/all_to_all | solution.py:284
  37.8 3.5 %all-to-all-start.2 = ((bf16[8,6,1536]{2,1,0:T(8,128)(2,1)}), bf16[8,6,1536]{2,1,0:T(8,128)(2,1)S(1)}, u32[]{:S(2)}, u32[]{:S(2)}) async-start(bf16[8,6,1536]{2,1,0:T(8,128)(2,1)} %broadcast_in_dim.34), calls=%async_computation.2 | async-start | bytes 393216 | tf_op jit(solution)/shard_map/all_to_all | solution.py:286
  41.3 1.3 fusion.1
  42.8 1.4 fusion
  44.2 4.8 %all-to-all-done.2 = bf16[8,6,1536]{2,1,0:T(8,128)(2,1)S(1)} async-done(((bf16[8,6,1536]{2,1,0:T(8,128)(2,1)}), bf16[8,6,1536]{2,1,0:T(8,128)(2,1)S(1)}, u32[]{:S(2)}, u32[]{:S(2)}) %all-to-all-start.2) | async-done | bytes 147488 | tf_op jit(solution)/shard_map/all_to_all | solution.py:286
  49.6 3.8 %all-to-all-start.3 = ((bf16[8,192,640]{2,1,0:T(8,128)(2,1)}), bf16[8,192,640]{2,1,0:T(8,128)(2,1)S(1)}, u32[]{:S(2)}, u32[]{:S(2)}) async-start(bf16[8,192,640]{2,1,0:T(8,128)(2,1)} %bitcast.55), calls=%async_computation.3 | async-start | bytes 3932160 | tf_op jit(solution)/shard_map/all_to_all | solution.py:291
  53.4 17.1 %collective-permute-done.5 = bf16[320,1536]{1,0:T(8,128)(2,1)} collective-permute-done((bf16[320,1536]{1,0:T(8,128)(2,1)}, bf16[320,1536]{1,0:T(8,128)(2,1)}, u32[]{:S(2)}, u32[]{:S(2)}) %collective-permute-start.5) | collective-permute-done | bytes 983072 | tf_op jit(solution)/shard_map/ppermute | solution.py:305
  70.5 1.6 broadcast_select_fusion.5
  72.1 1.5 pad_maximum_fusion.1.refs_2_
  76.0 0.8 dynamic_slice.29
  77.4 1.5 collective-permute-start.7
  78.9 3.6 %collective-permute-done.3 = bf16[8,6,1536]{2,1,0:T(8,128)(2,1)S(1)} collective-permute-done((bf16[8,6,1536]{2,1,0:T(8,128)(2,1)S(1)}, bf16[8,6,1536]{2,1,0:T(8,128)(2,1)S(1)}, u32[]{:S(2)}, u32[]{:S(2)}) %collective-permute-start.3) | collective-permute-done | bytes 147488 | tf_op jit(solution)/shard_map/ppermute | solution.py:41
  82.6 0.8 maximum_bitcast_fusion
  83.5 1.1 reshape.197.refs_0_
  85.2 0.8 copy.60
  86.0 1.1 reshape.200
  87.1 4.6 %absorb.1.qk_ref = bf16[2304,640]{1,0:T(8,128)(2,1)S(1)} custom-call(bf16[96,1536]{1,0:T(8,128)(2,1)S(1)} %reshape.197.refs_0_, bf16[96,1536]{1,0:T(8,128)(2,1)} %collective-permute-done.4.refs_1_, bf16[640,1536]{1,0:T(8,128)(2,1)} %pad_maximum_fusion.1.refs_2_, bf16[640,1536]{1,0:T(8,128)(2,1)} %collective-permute-done.6.refs_3_, ...), custom_call_target="tpu_custom_call" | custom-call | flops 377487360 | bytes 4521984 | tf_op jit(solution)/shard_map/absorb/pallas_call | solution.py:310
  91.7 1.6 copy-done.1
  93.3 2.8 %all-to-all-done.3.slab_ref = bf16[8,192,640]{2,1,0:T(8,128)(2,1)S(1)} async-done(((bf16[8,192,640]{2,1,0:T(8,128)(2,1)}), bf16[8,192,640]{2,1,0:T(8,128)(2,1)S(1)}, u32[]{:S(2)}, u32[]{:S(2)}) %all-to-all-start.3) | async-done | bytes 1966112 | tf_op jit(solution)/shard_map/all_to_all | solution.py:291
  96.2 1.8 %copy-done.2 = bf16[2304,640]{1,0:T(8,128)(2,1)S(1)} copy-done((bf16[2304,640]{1,0:T(8,128)(2,1)S(1)}, bf16[2304,640]{1,0:T(8,128)(2,1)}, u32[]{:S(2)}) %copy-start.2) | copy-done | bytes 2949144
  98.0 8.4 %scores.1 = bf16[8,80,256]{2,1,0:T(8,128)(2,1)} custom-call(bf16[2304,640]{1,0:T(8,128)(2,1)S(1)} %copy-done.2, s32[1,1536]{1,0:T(1,128)S(1)} %reshape.204.slot_ref, s32[1,128]{1,0:T(1,128)S(1)} %pad_bitcast_fusion.new_slot_ref, bf16[8,192,640]{2,1,0:T(8,128)(2,1)S(1)} %all-to-all-done.3.slab_ref, bf16[128,640]{1,0:T(8,128)(2,1)S(1)} %pad.14.new_ref), custom_call_target="tpu_custom_call" | custom-call | tf_op jit(solution)/shard_map/scores/pallas_call | solution.py:334
  106.4 3.6 %all-to-all-start.4 = ((bf16[8,80,256]{2,1,0:T(8,128)(2,1)}), bf16[8,80,256]{2,1,0:T(8,128)(2,1)S(1)}, u32[]{:S(2)}, u32[]{:S(2)}) async-start(bf16[8,80,256]{2,1,0:T(8,128)(2,1)} %scores.1), calls=%async_computation.4 | async-start | bytes 655360 | tf_op jit(solution)/shard_map/all_to_all | solution.py:341
  110.1 2.9 %broadcast_select_fusion.3 = (bf16[320,1536]{1,0:T(8,128)(2,1)}, bf16[320,1536]{1,0:T(8,128)(2,1)}) fusion(bf16[320,1536]{1,0:T(8,128)(2,1)} %param.16, bf16[320,1536]{1,0:T(8,128)(2,1)} %collective-permute-done.7, pred[]{:T(512)S(6)} %eq.46), kind=kLoop, calls=%fused_computation.21 | loop fusion | flops 983040 | bytes 3932161 | tf_op jit(solution)/shard_map/jit(_where)/select_n | solution.py:301
  113.0 7.4 %all-to-all-done.4 = bf16[8,80,256]{2,1,0:T(8,128)(2,1)S(1)} async-done(((bf16[8,80,256]{2,1,0:T(8,128)(2,1)}), bf16[8,80,256]{2,1,0:T(8,128)(2,1)S(1)}, u32[]{:S(2)}, u32[]{:S(2)}) %all-to-all-start.4) | async-done | bytes 327712 | tf_op jit(solution)/shard_map/all_to_all | solution.py:341
  120.8 0.8 broadcast_in_dim.63
  121.5 3.7 %all-to-all-start.5 = ((bf16[8,80,256]{2,1,0:T(8,128)(2,1)}), bf16[8,80,256]{2,1,0:T(8,128)(2,1)S(1)}, u32[]{:S(2)}, u32[]{:S(2)}) async-start(bf16[8,80,256]{2,1,0:T(8,128)(2,1)} %broadcast_in_dim.63), calls=%async_computation.5 | async-start | bytes 655360 | tf_op jit(solution)/shard_map/all_to_all | solution.py:359
  125.2 1.8 %broadcast_select_fusion.1 = (bf16[320,1536]{1,0:T(8,128)(2,1)S(1)}, bf16[320,1536]{1,0:T(8,128)(2,1)S(1)}) fusion(bf16[320,1536]{1,0:T(8,128)(2,1)} %collective-permute-done.8, bf16[320,1536]{1,0:T(8,128)(2,1)} %collective-permute-done.9, pred[]{:T(512)S(6)} %eq.46), kind=kLoop, calls=%fused_computation.19 | loop fusion | flops 983040 | bytes 3932161 | tf_op jit(solution)/shard_map/jit(_where)/select_n | solution.py:301
  127.3 2.1 %pad_maximum_fusion.2 = (bf16[640,1536]{1,0:T(8,128)(2,1)}, bf16[640,1536]{1,0:T(8,128)(2,1)}) fusion(bf16[320,1536]{1,0:T(8,128)(2,1)S(1)} %copy-done.6, bf16[320,1536]{1,0:T(8,128)(2,1)S(1)} %copy-done.5, bf16[320,1536]{1,0:T(8,128)(2,1)S(1)} %get-tuple-element.30, bf16[320,1536]{1,0:T(8,128)(2,1)S(1)} %get-tuple-element.29), kind=kLoop, calls=%fused_computation.10 | loop fusion | flops 7864320 | bytes 7864320 | tf_op jit(solution)/shard_map/concatenate | solution.py:300
  129.4 6.0 %all-to-all-done.5.w_ref = bf16[8,80,256]{2,1,0:T(8,128)(2,1)S(1)} async-done(((bf16[8,80,256]{2,1,0:T(8,128)(2,1)}), bf16[8,80,256]{2,1,0:T(8,128)(2,1)S(1)}, u32[]{:S(2)}, u32[]{:S(2)}) %all-to-all-start.5) | async-done | bytes 327712 | tf_op jit(solution)/shard_map/all_to_all | solution.py:359
  135.4 1.5 copy-done.3
  136.9 1.5 copy-done.4
  138.5 8.1 %values.1 = (bf16[96,1536]{1,0:T(8,128)(2,1)S(1)}, bf16[96,1536]{1,0:T(8,128)(2,1)S(1)}, f32[96,128]{1,0:T(8,128)S(1)}) custom-call(bf16[8,80,256]{2,1,0:T(8,128)(2,1)S(1)} %all-to-all-done.5.w_ref, s32[1,1664]{1,0:T(1,128)S(1)} %pad_add_fusion.slot_ref, f32[1,640]{1,0:T(1,128)S(1)} %reshape.198.refs_4_.gain_ref, ...), custom_call_target="tpu_custom_call" | custom-call | tf_op jit(solution)/shard_map/values/pallas_call | solution.py:365
  147.2 1.1 collective-permute-done.11.theirs_d_ref
  148.9 17.3 %all_to_all.35 = bf16[16,8,1536]{2,1,0:T(8,128)(2,1)S(1)} all-to-all(bf16[16,8,1536]{2,1,0:T(8,128)(2,1)S(1)} %join.1), channel_id=1, replica_groups=mesh['seq'=16,'tp'=2] {'seq'}, dimensions={0} | all-to-all | bytes 786432 | tf_op jit(solution)/shard_map/all_to_all | solution.py:403
  (105 shorter events, 10.2 us)
Async XLA Ops:
  0.0 20.1 %copy-start = (bf16[320,1536]{1,0:T(8,128)(2,1)S(1)}, bf16[320,1536]{1,0:T(8,128)(2,1)}, u32[]{:S(2)}) copy-start(bf16[320,1536]{1,0:T(8,128)(2,1)} %param.17) | copy-start | bytes 2949124
  0.9 2.1 %collective-permute-start = (bf16[6,2560]{1,0:T(8,128)(2,1)S(1)}, bf16[6,2560]{1,0:T(8,128)(2,1)S(1)}, u32[]{:S(2)}, u32[]{:S(2)}) collective-permute-start(bf16[6,2560]{1,0:T(8,128)(2,1)S(1)} %reshape.189), channel_id=1, source_target_pairs={{0,1},{1,0},{2,3},{3,2},{4,5},{5,4},{6,7},{7,6},{8,9},{9,8},{10,11... | collective-permute-start | bytes 92168 | tf_op jit(solution)/shard_map/ppermute | solution.py:235
  4.1 15.6 %all-to-all-start = ((bf16[16,7,320]{2,1,0:T(8,128)(2,1)}), bf16[16,7,320]{2,1,0:T(8,128)(2,1)S(1)}, u32[]{:S(2)}, u32[]{:S(2)}) async-start(bf16[16,7,320]{2,1,0:T(8,128)(2,1)} %pad_maximum_fusion.5), calls=%async_computation | async-start | bytes 196608 | tf_op jit(solution)/shard_map/all_to_all | solution.py:267
  14.3 27.0 %collective-permute-start.2 = (bf16[192,2560]{1,0:T(8,128)(2,1)}, bf16[192,2560]{1,0:T(8,128)(2,1)}, u32[]{:S(2)}, u32[]{:S(2)}) collective-permute-start(bf16[192,2560]{1,0:T(8,128)(2,1)} %dynamic-slice_bitcast_fusion), channel_id=1, source_target_pairs={{0,1},{1,0},{2,3},{3,2},{4,5},{5,4},{6,7},{7,6},{8,9},{9,8},{10,11... | collective-permute-start | bytes 2949128 | tf_op jit(solution)/shard_map/ppermute | solution.py:242
  20.5 20.8 %copy-start.7 = (bf16[384,2560]{1,0:T(8,128)(2,1)S(1)}, bf16[384,2560]{1,0:T(8,128)(2,1)}, u32[]{:S(2)}) copy-start(bf16[384,2560]{1,0:T(8,128)(2,1)} %param.9) | copy-start | bytes 5898244
  21.4 15.6 %all-to-all-start.1 = ((bf16[16,6,1536]{2,1,0:T(8,128)(2,1)}), bf16[16,6,1536]{2,1,0:T(8,128)(2,1)S(1)}, u32[]{:S(2)}, u32[]{:S(2)}) async-start(bf16[16,6,1536]{2,1,0:T(8,128)(2,1)} %copy.57), calls=%async_computation.1 | async-start | bytes 786432 | tf_op jit(solution)/shard_map/all_to_all | solution.py:284
  25.0 5.0 %collective-permute-start.1 = (bf16[96,320]{1,0:T(8,128)(2,1)S(1)}, bf16[96,320]{1,0:T(8,128)(2,1)}, u32[]{:S(2)}, u32[]{:S(2)}) collective-permute-start(bf16[96,320]{1,0:T(8,128)(2,1)S(1)} %reshape.194), channel_id=1, source_target_pairs={{0,2},{2,0},{4,6},{6,4},{8,10},{10,8},{12,14},{14,12},{16,18},{18,... | collective-permute-start | bytes 184328 | tf_op jit(solution)/shard_map/ppermute | solution.py:41
  37.8 11.3 %all-to-all-start.2 = ((bf16[8,6,1536]{2,1,0:T(8,128)(2,1)}), bf16[8,6,1536]{2,1,0:T(8,128)(2,1)S(1)}, u32[]{:S(2)}, u32[]{:S(2)}) async-start(bf16[8,6,1536]{2,1,0:T(8,128)(2,1)} %broadcast_in_dim.34), calls=%async_computation.2 | async-start | bytes 393216 | tf_op jit(solution)/shard_map/all_to_all | solution.py:286
  49.0 21.4 %collective-permute-start.5 = (bf16[320,1536]{1,0:T(8,128)(2,1)}, bf16[320,1536]{1,0:T(8,128)(2,1)}, u32[]{:S(2)}, u32[]{:S(2)}) collective-permute-start(bf16[320,1536]{1,0:T(8,128)(2,1)} %param.15), channel_id=1, source_target_pairs={{0,2},{2,0},{4,6},{6,4},{8,10},{10,8},{12,14},{14,12},{16,18},{18,... | collective-permute-start | bytes 2949128 | tf_op jit(solution)/shard_map/ppermute | solution.py:305
  49.6 46.6 %all-to-all-start.3 = ((bf16[8,192,640]{2,1,0:T(8,128)(2,1)}), bf16[8,192,640]{2,1,0:T(8,128)(2,1)S(1)}, u32[]{:S(2)}, u32[]{:S(2)}) async-start(bf16[8,192,640]{2,1,0:T(8,128)(2,1)} %bitcast.55), calls=%async_computation.3 | async-start | bytes 3932160 | tf_op jit(solution)/shard_map/all_to_all | solution.py:291
  73.5 11.7 %copy-start.8 = (bf16[2,96,320]{2,1,0:T(8,128)(2,1)S(1)}, bf16[2,96,320]{2,1,0:T(8,128)(2,1)}, u32[]{:S(2)}) copy-start(bf16[2,96,320]{2,1,0:T(8,128)(2,1)} %pad_maximum_fusion.4) | copy-start | bytes 368644
  73.6 13.6 %collective-permute-start.6 = (bf16[640,1536]{1,0:T(8,128)(2,1)}, bf16[640,1536]{1,0:T(8,128)(2,1)}, u32[]{:S(2)}, u32[]{:S(2)}) collective-permute-start(bf16[640,1536]{1,0:T(8,128)(2,1)} %pad_maximum_fusion.1.refs_2_), channel_id=1, source_target_pairs={{0,1},{1,0},{2,3},{3,2},{4,5},{5,4},{6,7},{7,6},{8,9},{9,8},{10,11... | collective-permute-start | bytes 5898248 | tf_op jit(solution)/shard_map/ppermute | solution.py:235
  74.9 7.7 %collective-permute-start.3 = (bf16[8,6,1536]{2,1,0:T(8,128)(2,1)S(1)}, bf16[8,6,1536]{2,1,0:T(8,128)(2,1)S(1)}, u32[]{:S(2)}, u32[]{:S(2)}) collective-permute-start(bf16[8,6,1536]{2,1,0:T(8,128)(2,1)S(1)} %all-to-all-done.2), channel_id=1, source_target_pairs={{0,2},{2,0},{4,6},{6,4},{8,10},{10,8},{12,14},{14,12},{16,18},{18,... | collective-permute-start | bytes 442376 | tf_op jit(solution)/shard_map/ppermute | solution.py:41
  77.4 29.0 %collective-permute-start.7 = (bf16[320,1536]{1,0:T(8,128)(2,1)}, bf16[320,1536]{1,0:T(8,128)(2,1)}, u32[]{:S(2)}, u32[]{:S(2)}) collective-permute-start(bf16[320,1536]{1,0:T(8,128)(2,1)} %param.16), channel_id=1, source_target_pairs={{0,2},{2,0},{4,6},{6,4},{8,10},{10,8},{12,14},{14,12},{16,18},{18,... | collective-permute-start | bytes 2949128 | tf_op jit(solution)/shard_map/ppermute | solution.py:305
  84.6 2.6 %collective-permute-start.4 = (bf16[96,1536]{1,0:T(8,128)(2,1)S(1)}, bf16[96,1536]{1,0:T(8,128)(2,1)}, u32[]{:S(2)}, u32[]{:S(2)}) collective-permute-start(bf16[96,1536]{1,0:T(8,128)(2,1)S(1)} %reshape.197.refs_0_), channel_id=1, source_target_pairs={{0,1},{1,0},{2,3},{3,2},{4,5},{5,4},{6,7},{7,6},{8,9},{9,8},{10,11... | collective-permute-start | bytes 884744 | tf_op jit(solution)/shard_map/ppermute | solution.py:235
  84.7 40.5 %collective-permute-start.8 = (bf16[320,1536]{1,0:T(8,128)(2,1)}, bf16[320,1536]{1,0:T(8,128)(2,1)}, u32[]{:S(2)}, u32[]{:S(2)}) collective-permute-start(bf16[320,1536]{1,0:T(8,128)(2,1)} %param.16), channel_id=1, source_target_pairs={{0,1},{1,0},{2,3},{3,2},{4,5},{5,4},{6,7},{7,6},{8,9},{9,8},{10,11... | collective-permute-start | bytes 2949128 | tf_op jit(solution)/shard_map/ppermute | solution.py:235
  91.7 1.6 copy-start.1
  96.2 1.8 %copy-start.2 = (bf16[2304,640]{1,0:T(8,128)(2,1)S(1)}, bf16[2304,640]{1,0:T(8,128)(2,1)}, u32[]{:S(2)}) copy-start(bf16[2304,640]{1,0:T(8,128)(2,1)} %copy-done.1) | copy-start | bytes 8847364
  106.4 14.1 %all-to-all-start.4 = ((bf16[8,80,256]{2,1,0:T(8,128)(2,1)}), bf16[8,80,256]{2,1,0:T(8,128)(2,1)S(1)}, u32[]{:S(2)}, u32[]{:S(2)}) async-start(bf16[8,80,256]{2,1,0:T(8,128)(2,1)} %scores.1), calls=%async_computation.4 | async-start | bytes 655360 | tf_op jit(solution)/shard_map/all_to_all | solution.py:341
  110.0 10.5 %copy-start.9 = (pred[256]{0:T(512)(128)(4,1)S(1)}, pred[256]{0:T(512)(128)(4,1)}, u32[]{:S(2)}) copy-start(pred[256]{0:T(512)(128)(4,1)} %get-tuple-element.51) | copy-start | bytes 772
  110.0 10.5 %copy-start.10 = (pred[256]{0:T(512)(128)(4,1)S(1)}, pred[256]{0:T(512)(128)(4,1)}, u32[]{:S(2)}) copy-start(pred[256]{0:T(512)(128)(4,1)} %get-tuple-element.52) | copy-start | bytes 772
  110.0 10.5 %copy-start.11 = (s32[256]{0:T(256)S(1)}, s32[256]{0:T(256)}, u32[]{:S(2)}) copy-start(s32[256]{0:T(256)} %and_select_fusion.1) | copy-start | bytes 3076
  110.0 10.5 %copy-start.12 = (s32[72]{0:T(128)S(1)}, s32[72]{0:T(128)}, u32[]{:S(2)}) copy-start(s32[72]{0:T(128)} %and_select_fusion) | copy-start | bytes 868
  110.0 10.6 %copy-start.13 = (bf16[80]{0:T(256)(128)(2,1)S(1)}, bf16[80]{0:T(256)(128)(2,1)}, u32[]{:S(2)}) copy-start(bf16[80]{0:T(256)(128)(2,1)} %pad.24.clone) | copy-start | bytes 484
  110.0 15.2 %collective-permute-start.9 = (bf16[320,1536]{1,0:T(8,128)(2,1)}, bf16[320,1536]{1,0:T(8,128)(2,1)}, u32[]{:S(2)}, u32[]{:S(2)}) collective-permute-start(bf16[320,1536]{1,0:T(8,128)(2,1)} %collective-permute-done.7), channel_id=1, source_target_pairs={{0,1},{1,0},{2,3},{3,2},{4,5},{5,4},{6,7},{7,6},{8,9},{9,8},{10,11... | collective-permute-start | bytes 2949128 | tf_op jit(solution)/shard_map/ppermute | solution.py:235
  121.5 13.8 %all-to-all-start.5 = ((bf16[8,80,256]{2,1,0:T(8,128)(2,1)}), bf16[8,80,256]{2,1,0:T(8,128)(2,1)S(1)}, u32[]{:S(2)}, u32[]{:S(2)}) async-start(bf16[8,80,256]{2,1,0:T(8,128)(2,1)} %broadcast_in_dim.63), calls=%async_computation.5 | async-start | bytes 655360 | tf_op jit(solution)/shard_map/all_to_all | solution.py:359
  125.2 1.8 %copy-start.5 = (bf16[320,1536]{1,0:T(8,128)(2,1)S(1)}, bf16[320,1536]{1,0:T(8,128)(2,1)}, u32[]{:S(2)}) copy-start(bf16[320,1536]{1,0:T(8,128)(2,1)} %get-tuple-element.31) | copy-start | bytes 2949124
  125.2 2.1 %copy-start.6 = (bf16[320,1536]{1,0:T(8,128)(2,1)S(1)}, bf16[320,1536]{1,0:T(8,128)(2,1)}, u32[]{:S(2)}) copy-start(bf16[320,1536]{1,0:T(8,128)(2,1)} %get-tuple-element.32) | copy-start | bytes 2949124
  135.4 1.5 copy-start.3
  136.9 1.5 copy-start.4
  146.6 1.7 %collective-permute-start.10 = (bf16[96,1536]{1,0:T(8,128)(2,1)S(1)}, bf16[96,1536]{1,0:T(8,128)(2,1)S(1)}, u32[]{:S(2)}, u32[]{:S(2)}) collective-permute-start(bf16[96,1536]{1,0:T(8,128)(2,1)S(1)} %get-tuple-element.23), channel_id=1, source_target_pairs={{0,1},{1,0},{2,3},{3,2},{4,5},{5,4},{6,7},{7,6},{8,9},{9,8},{10,11... | collective-permute-start | bytes 884744 | tf_op jit(solution)/shard_map/ppermute | solution.py:390
  146.7 1.6 collective-permute-start.11
